TPU v7x, 256 devices: a whole 4x4x8 slice. The times are simulated.
256 devices in a mesh: store: 32 (over z, y), head: 8 (over x, core).
Axes of the slice: x: 4, y: 4, z: 8, core: 2. Of those that a mesh axis runs over, the one named last changes fastest.
Arguments:
- queries: bfloat16 [32768, 4096], P('store', 'head'), may hold values from -7.2 to 7.2
- neighbour_ids: int32 [512, 2], P('store'), may hold values from 0 to 255, as said below
- neighbour_kv: bfloat16 [256, 128, 2, 4096], P('store', None, None, 'head'), may hold values from -7.2 to 7.2
- out_weight: bfloat16 [4096, 8192], P('head'), may hold values from -0.375 to 0.375
Outputs:
- mixed: bfloat16 [32768, 8192], P('store', 'head')
Inputs may be any that keep to these rules, and one draw needn't show every extreme that they name: `neighbour_ids`: the two neighbours of a segment differ. The 32 ids of the segments of one index of store (aligned blocks of 16 rows) are all different, and at most 2 of them lie in the ids of one holder (ids h * 8 to h * 8 + 7); every such block reaches 2 for some holder.
All inputs are finite; a program needn't handle non-finite values.
Results may differ from a plain program's by a relative error of at most 0.0159.
Values may be sent and summed in bfloat16 or wider, within the bound.
No kernel may reach another device: no remote copies, remote signals or barrier semaphores. Data moves between devices by JAX's collectives and lax.ppermute only.
A program may use at most 128 MiB of HBM per device.

v0:
```python
import jax
import jax.numpy as jnp
from jax import lax
from jax.sharding import PartitionSpec as P

DH = 128


def body(queries, neighbour_ids, neighbour_kv, out_weight):
    stores = lax.axis_size("store")
    segments = neighbour_ids.shape[0]
    held_count = neighbour_kv.shape[0]
    near_len = neighbour_kv.shape[1]
    local_cols = neighbour_kv.shape[3]
    heads_local = local_cols // DH
    seg_len = queries.shape[0] // segments
    capacity = max(2, 4 * segments // stores)
    references = neighbour_ids.reshape(-1)
    ref_count = references.shape[0]
    holder = references // held_count
    slot_index = references % held_count
    order = jnp.arange(ref_count)
    earlier = (holder[:, None] == holder[None, :]) & (order[None, :] < order[:, None])
    rank_at = jnp.sum(earlier.astype(jnp.int32), axis=1)
    holder_hit = holder[:, None] == jnp.arange(stores)[None, :]
    rank_hit = rank_at[:, None] == jnp.arange(capacity)[None, :]
    placed = holder_hit[:, :, None] & rank_hit[:, None, :]
    requests = jnp.sum(jnp.where(placed, slot_index[:, None, None] + 1, 0), axis=0) - 1
    score_scale = DH ** (-0.5)
    kv_rows = neighbour_kv[
        jnp.maximum(lax.all_to_all(requests, "store", split_axis=0, concat_axis=0, tiled=True), 0)
    ]
    fetched = lax.all_to_all(kv_rows, "store", split_axis=0, concat_axis=0, tiled=True)
    picked = fetched[holder, rank_at].reshape(segments, 2, near_len, 2, heads_local, DH)
    query_segs = queries.reshape(segments, seg_len, heads_local, DH)
    scores = (
        jnp.einsum(
            "cqhd,cjkhd->chqjk", query_segs, picked[:, :, :, 0], preferred_element_type=jnp.float32
        )
        * score_scale
    )
    part_max = jnp.max(scores, axis=-1)
    weights = jnp.exp(scores - part_max[..., None])
    part_total = jnp.sum(weights, axis=-1)
    part_sum = jnp.einsum(
        "chqjk,cjkhd->chqjd",
        weights.astype(jnp.bfloat16),
        picked[:, :, :, 1],
        preferred_element_type=jnp.float32,
    )
    row_max = jnp.max(part_max, axis=-1, keepdims=True)
    factor = jnp.exp(part_max - row_max)
    merged_sum = jnp.sum(part_sum * factor[..., None], axis=3)
    merged_total = jnp.sum(part_total * factor, axis=-1)
    context = jnp.transpose(merged_sum / merged_total[..., None], (0, 2, 1, 3))
    context = context.reshape(segments * seg_len, local_cols).astype(jnp.bfloat16)
    partial_value = jnp.dot(context, out_weight, preferred_element_type=jnp.float32)
    return lax.psum_scatter(
        partial_value.astype(jnp.bfloat16), "head", scatter_dimension=1, tiled=True
    )


def solution(mesh):
    in_specs = (
        P("store", "head"),
        P("store", None),
        P("store", None, None, "head"),
        P("head", None),
    )
    out_specs = P("store", "head")
    return jax.shard_map(body, mesh=mesh, in_specs=in_specs, out_specs=out_specs, check_vma=False)
```

profile of v0, /device:TPU:1, one launch (start us, length us, event | category | flops | bytes accessed | tf_op | source)
XLA Modules:
  0.0 643.9 jit_solution(4688516153259229634)
XLA Ops:
  6.5 0.9 copy.32
  7.4 0.1 reshape.232
  7.5 0.2 convert_reduce_fusion
  7.7 0.1 iota_compare_fusion.1
  7.8 0.1 select_reduce_fusion
  7.9 0.1 copy.33
  8.0 20.4 %all_to_all.11 = s32[32,1,2]{2,1,0:T(1,128)S(1)} all-to-all(s32[32,1,2]{2,1,0:T(1,128)S(1)} %copy.33), channel_id=1, replica_groups=mesh['store'=32,'head'=8] {'store'}, dimensions={0} | all-to-all | bytes 512 | tf_op jit(solution)/shard_map/all_to_all | solution.py:31
  28.4 0.1 maximum_reduce_fusion
  28.5 0.1 reshape.238
  28.6 34.9 %gather_fusion = bf16[64,128,2,512]{3,2,1,0:T(2,128)(2,1)} fusion(bf16[8,128,2,512]{3,2,1,0:T(2,128)(2,1)S(1)} %copy-done, s32[1024]{0:T(1024)S(1)} %pad_clamp_fusion), kind=kCustom, calls=%fused_computation | custom fusion | bytes 33554688 | tf_op jit(solution)/shard_map/gather | solution.py:30
  63.5 15.8 %copy.34 = bf16[64,128,2,512]{3,1,2,0:T(8,128)(2,1)} copy(bf16[64,128,2,512]{3,2,1,0:T(2,128)(2,1)} %gather_fusion) | data formatting | bytes 33554432 | tf_op jit(solution)/shard_map/gather | solution.py:30
  79.3 5.3 all-to-all-start.1
  84.6 0.2 reduce-scatter.2.cloned.1.call-start
  84.8 0.1 reshape.233
  84.9 0.3 reshape.235
  85.2 379.9 %all-to-all-done.1 = bf16[32,2,128,2,512]{4,2,3,1,0:T(8,128)(2,1)} async-done(((bf16[32,2,128,2,512]{4,2,3,1,0:T(8,128)(2,1)}), bf16[32,2,128,2,512]{4,2,3,1,0:T(8,128)(2,1)}, u32[]{:S(2)}, u32[]{:S(2)}) %all-to-all-start.1) | async-done | bytes 16777248 | tf_op jit(solution)/shard_map/all_to_all | solution.py:33
  465.1 10.9 %gather_fusion.1 = bf16[32,128,2,512]{3,1,2,0:T(8,128)(2,1)} fusion(bf16[32,2,128,2,512]{4,2,3,1,0:T(8,128)(2,1)} %all-to-all-done.1, s32[32]{0:T(128)S(1)} %fusion.26), kind=kCustom, calls=%fused_computation.1 | custom fusion | bytes 16777472 | tf_op jit(solution)/shard_map/gather | solution.py:34
  476.1 11.9 %copy.36 = bf16[32,128,2,512]{1,3,2,0:T(8,128)(2,1)} copy(bf16[32,128,2,512]{3,1,2,0:T(8,128)(2,1)} %gather_fusion.1) | data formatting | bytes 16777216 | tf_op jit(solution)/shard_map/gather | solution.py:34
  488.0 6.0 fusion.28
  494.0 6.4 copy.44
  500.4 6.4 copy.45
  506.8 3.9 bitcast_reduce_fusion.1
  510.7 3.0 fusion.6
  513.7 0.1 multiply_reduce_fusion
  513.9 0.0 slice-start.1
  513.9 2.7 fusion
  516.6 0.7 fusion.9
  517.3 0.9 copy.40
  518.2 12.0 %convolution_convert_fusion = bf16[1024,8192]{1,0:T(8,128)(2,1)} fusion(bf16[512,8192]{1,0:T(8,128)(2,1)S(1)} %bitcast.55, bf16[128,8,4,128]{3,2,1,0:T(4,128)(2,1)S(1)} %bitcast.52), kind=kOutput, calls=%fused_computation.2 | convolution fusion | flops 8598323200 | bytes 26214400 | tf_op jit(solution)/shard_map/dot_general | solution.py:57
  530.3 0.0 reduce-scatter.2.cloned.1.call-update
  530.3 0.0 copy-start.1
  530.3 106.8 %reduce-scatter.2.cloned.1.call-done = bf16[1024,1024]{1,0:T(8,128)(2,1)} async-done(((bf16[1024,8192]{1,0:T(8,128)(2,1)}), bf16[1024,1024]{1,0:T(8,128)(2,1)}) %reduce-scatter.2.cloned.1.call-update) | async-done | bytes 2097168 | tf_op jit(solution)/shard_map/reduce_scatter | solution.py:58
  (16 shorter events, 0.1 us)
Async XLA Ops:
  6.5 22.1 %copy-start = (bf16[8,128,2,512]{3,2,1,0:T(2,128)(2,1)S(1)}, bf16[8,128,2,512]{3,2,1,0:T(2,128)(2,1)}, u32[]{:S(2)}) copy-start(bf16[8,128,2,512]{3,2,1,0:T(2,128)(2,1)} %param.6) | copy-start | bytes 6291460
  79.3 5.6 copy-start.3
  79.3 385.8 %all-to-all-start.1 = ((bf16[32,2,128,2,512]{4,2,3,1,0:T(8,128)(2,1)}), bf16[32,2,128,2,512]{4,2,3,1,0:T(8,128)(2,1)}, u32[]{:S(2)}, u32[]{:S(2)}) async-start(bf16[32,2,128,2,512]{4,2,3,1,0:T(8,128)(2,1)} %bitcast.49), calls=%async_computation.1 | async-start | bytes 33554432 | tf_op jit(solution)/shard_map/all_to_all | solution.py:33
  84.6 552.4 %reduce-scatter.2.cloned.1.call-start = ((), (), s32[]{:S(2)}) async-start(), calls=%async_computation.3 | async-start | bytes 18874368 | tf_op jit(solution)/shard_map/reduce_scatter | solution.py:58
  510.7 3.2 copy-start.2
  513.9 4.4 slice-start
  513.9 4.4 slice-start.1
  530.3 106.8 %copy-start.1 = (bf16[8,128,2,512]{3,2,1,0:T(2,128)(2,1)S(1)}, bf16[8,128,2,512]{3,2,1,0:T(2,128)(2,1)}, u32[]{:S(2)}) copy-start(bf16[8,128,2,512]{3,2,1,0:T(2,128)(2,1)} %param.6) | copy-start | bytes 6291460
Sparse Core Ops, SparseCore 0:
  530.4 106.6 reduce-scatter.1
where the time goes:
time: 645 us; the launch traced here: 644 us
  waiting for transfers between devices  487 us (76%)
  local copies, waits for them, and re-layouts  94.8 us (15%)
  blocking collectives  20.4 us (3%)
  matrix products  18.6 us (3%)
  between operations  13.6 us (2%)
    all_to_all x1, waiting for transfers between devices, body(): lax.all_to_all(kv_rows, 'store', split_axis=0, concat_axis=0, tiled=True)  380 us
    reduce_scatter x1, waiting for transfers between devices, body(): lax.psum_scatter(partial_value.astype(jnp.bfloat16), 'head', scatter_dime...  107 us
    gather x2, local copies, waits for them, and re-layouts, body(): neighbour_kv[jnp.maximum(lax.all_to_all(requests, 'store', split_axis=0,...  50.7 us
    gather x2, local copies, waits for them, and re-layouts, body(): fetched[holder, rank_at].reshape(segments, 2, near_len, 2, heads_local, DH)  22.8 us
    all_to_all x1, blocking collectives, body(): lax.all_to_all(requests, 'store', split_axis=0, concat_axis=0, tiled=True)  20.4 us
    unnamed x15, local copies, waits for them, and re-layouts  13.7 us
  transfers between devices with their start and end apart: 2, of which 2 were waited for; matrix products, arithmetic and copies ran while one was open for 0% of the time, Pallas kernels for 0%

commit v1 on v0

v1 whole, which is shorter than its diff:
```python
import functools

import jax
import jax.numpy as jnp
import numpy as np
from jax import lax
from jax.experimental import pallas as pl
from jax.experimental.pallas import tpu as pltpu
from jax.sharding import Mesh, PartitionSpec as P

NZ, NY, NX, NC = 8, 4, 4, 2
DH = 128
SEG = 64
SEGS = 16
REFS = 2 * SEGS
NB_DEV = 8
NB_LEN = 128
ROW_NB = NY * NB_DEV
SLOTS = 8
TILES = SLOTS // 2
OUT_ROWS = TILES * DH + 16
MB = 1 << 20


def attn_kernel(ids_ref, me_ref, q_ref, kv_ref, out_ref, slot_ref):
    zi = pl.program_id(0)
    zme = me_ref[0]
    count = jnp.int32(0)
    for i in range(REFS):
        slot_ref[i] = jnp.int32(0)
    for i in range(REFS):
        hit = ids_ref[zi * REFS + i] // ROW_NB == zme
        slot_ref[count] = jnp.int32(i)
        count = count + hit.astype(jnp.int32)
    low = lax.broadcasted_iota(jnp.int32, (1, 2 * SEG), 1) < SEG
    his, mids, los = [], [], []
    for t in range(TILES):
        queries, keys, values = [], [], []
        for half in range(2):
            ref = slot_ref[2 * t + half]
            nb = ids_ref[zi * REFS + ref] % ROW_NB
            start = pl.multiple_of((ref // 2) * SEG, SEG)
            queries.append(q_ref[pl.ds(start, SEG), :])
            yi, at = nb // NB_DEV, nb % NB_DEV
            keys.append(kv_ref[yi, 0, 0, at])
            values.append(kv_ref[yi, 0, 1, at])
        pair = jnp.concatenate(queries, axis=0)
        nt = (((1,), (1,)), ((), ()))
        s0 = lax.dot_general(keys[0], pair, nt, preferred_element_type=jnp.float32)
        s1 = lax.dot_general(keys[1], pair, nt, preferred_element_type=jnp.float32)
        scores = jnp.where(low, s0, s1) * (DH**-0.5)
        top = jnp.max(scores, axis=0, keepdims=True)
        weights = jnp.exp(scores - top)
        total = jnp.sum(weights, axis=0, keepdims=True)
        rounded = weights.astype(jnp.bfloat16)
        o0 = jnp.dot(values[0], rounded, preferred_element_type=jnp.float32)
        o1 = jnp.dot(values[1], rounded, preferred_element_type=jnp.float32)
        out = jnp.where(low, o0, o1) * (1.0 / total)
        out_ref[0, t * DH : (t + 1) * DH, :] = out.astype(jnp.bfloat16)
        lse = top + jnp.log(total)
        hi = lse.astype(jnp.bfloat16).astype(jnp.float32)
        mid = (lse - hi).astype(jnp.bfloat16).astype(jnp.float32)
        his.append(hi)
        mids.append(mid)
        los.append(lse - hi - mid)
    tail = jnp.concatenate(his + mids + los + [jnp.zeros((4, 2 * SEG), jnp.float32)], axis=0)
    out_ref[0, TILES * DH :, :] = tail.astype(jnp.bfloat16)


def attend(ids_all, zme, q_all, kv_all, hh):
    return pl.pallas_call(
        attn_kernel,
        grid_spec=pltpu.PrefetchScalarGridSpec(
            num_scalar_prefetch=2,
            grid=(NZ,),
            in_specs=[
                pl.BlockSpec((SEGS * SEG, DH), lambda z, *_: (z, hh)),
                pl.BlockSpec(
                    (NY, 1, 2, NB_DEV, DH, DH), lambda z, *_: (0, hh, 0, 0, 0, 0)
                ),
            ],
            out_specs=pl.BlockSpec((1, OUT_ROWS, 2 * SEG), lambda z, *_: (z, 0, 0)),
            scratch_shapes=[pltpu.SMEM((2 * REFS,), jnp.int32)],
        ),
        out_shape=jax.ShapeDtypeStruct((NZ, OUT_ROWS, 2 * SEG), jnp.bfloat16),
        compiler_params=pltpu.CompilerParams(vmem_limit_bytes=24 * MB),
        cost_estimate=pl.CostEstimate(
            flops=32 * 4 * 2 * DH**3 * 4, bytes_accessed=8 * MB, transcendentals=32 * DH * DH
        ),
        name="attend",
    )(ids_all, zme, q_all, kv_all)


def merge_kernel(ids_ref, part_ref, out_ref, lse_ref, place_ref, count_ref):
    for z in range(NZ):
        count_ref[z] = jnp.int32(0)
        tail = part_ref[z, TILES * DH :, :].astype(jnp.float32)
        lse_ref[z] = tail[0:4] + tail[4:8] + tail[8:12]
    for i in range(REFS):
        row = ids_ref[i] // ROW_NB
        rank = count_ref[row]
        count_ref[row] = rank + 1
        place_ref[i] = row * SLOTS + rank
    low = lax.broadcasted_iota(jnp.int32, (1, 2 * SEG), 1) < SEG
    for p in range(SEGS // 2):
        sums, lses = [], []
        for j in range(2):
            halves_o, halves_l = [], []
            for side in range(2):
                place = place_ref[2 * (2 * p + side) + j]
                z, rank = place // SLOTS, place % SLOTS
                tile, half = rank // 2, rank % 2
                start = pl.multiple_of(tile * DH, DH)
                part = part_ref[z, pl.ds(start, DH), :].astype(jnp.float32)
                lse = lse_ref[z, pl.ds(tile, 1), :]
                shift = jnp.where(half == side, 0, SEG)
                halves_o.append(pltpu.roll(part, shift, 1))
                halves_l.append(pltpu.roll(lse, shift, 1))
            sums.append(jnp.where(low, halves_o[0], halves_o[1]))
            lses.append(jnp.where(low, halves_l[0], halves_l[1]))
        top = jnp.maximum(lses[0], lses[1])
        f0, f1 = jnp.exp(lses[0] - top), jnp.exp(lses[1] - top)
        scale = 1.0 / (f0 + f1)
        context = ((f0 * scale) * sums[0] + (f1 * scale) * sums[1]).astype(jnp.bfloat16)
        for x in range(NX):
            out_ref[x, :, p * 2 * SEG : (p + 1) * 2 * SEG] = context


def merge(ids, parts):
    return pl.pallas_call(
        merge_kernel,
        grid_spec=pltpu.PrefetchScalarGridSpec(
            num_scalar_prefetch=1,
            grid=(),
            in_specs=[pl.BlockSpec(memory_space=pltpu.VMEM)],
            out_specs=pl.BlockSpec(memory_space=pltpu.VMEM),
            scratch_shapes=[
                pltpu.VMEM((NZ, TILES, 2 * SEG), jnp.float32),
                pltpu.SMEM((REFS,), jnp.int32),
                pltpu.SMEM((NZ,), jnp.int32),
            ],
        ),
        out_shape=jax.ShapeDtypeStruct((NX, DH, SEGS * SEG), jnp.bfloat16),
        compiler_params=pltpu.CompilerParams(vmem_limit_bytes=24 * MB),
        cost_estimate=pl.CostEstimate(
            flops=4 * DH * SEGS * SEG, bytes_accessed=3 * MB, transcendentals=2 * SEGS * SEG
        ),
        name="merge",
    )(ids, parts)


def body(queries, neighbour_ids, neighbour_kv, out_weight):
    heads = queries.shape[1] // DH
    zme = lax.axis_index("z").astype(jnp.int32).reshape(1)
    cme = lax.axis_index("core")
    ids = neighbour_ids.reshape(-1)
    ids_all = lax.all_gather(ids, "z", tiled=True)
    cols = out_weight.shape[1] // (NX * NC)

    def both(value):
        return jnp.broadcast_to(value[None], (NY, *value.shape))

    q_all, kv_all = [], []
    for pair in range(heads // 2):
        at = slice(pair * 2 * DH, (pair + 1) * 2 * DH)
        q_all.append(lax.all_gather(queries[:, at], "z", tiled=True))
    for pair in range(heads // 2):
        at = slice(pair * 2 * DH, (pair + 1) * 2 * DH)
        block = neighbour_kv[:, :, :, at].reshape(NB_DEV, NB_LEN, 2, 2, DH)
        keys = jnp.transpose(block[:, :, 0], (2, 0, 1, 3))
        values = jnp.transpose(block[:, :, 1], (2, 0, 3, 1))
        own = jnp.stack([keys, values], axis=1)
        kv_all.append(lax.all_to_all(both(own), "y", 0, 0, tiled=True))
    shares = jnp.transpose(out_weight.reshape(-1, NX, NC * cols), (1, 0, 2))
    plane = lax.all_to_all(shares, "x", 0, 0, tiled=True)
    plane = plane.reshape(NX, -1, NC, cols)
    w_own = lax.dynamic_index_in_dim(plane, cme, 2, keepdims=False)
    w_send = lax.dynamic_index_in_dim(plane, 1 - cme, 2, keepdims=False)
    swap = [(0, 1), (1, 0)]
    w_other = lax.ppermute(w_send, "core", swap)

    contract = (((0,), (0,)), ((), ()))
    total = None
    for head in range(heads):
        parts = attend(ids_all, zme, q_all[head // 2], kv_all[head // 2], head % 2)
        back = lax.all_to_all(parts, "z", 0, 0, tiled=True)
        context = merge(ids, back)
        gathered = lax.all_to_all(context, "x", 0, 0, tiled=True)
        other = lax.ppermute(gathered, "core", swap)
        rows = slice(head * DH, (head + 1) * DH)
        for ctx, weight in ((gathered, w_own), (other, w_other)):
            term = lax.dot_general(
                ctx.reshape(NX * DH, -1),
                weight[:, rows].reshape(NX * DH, cols),
                contract,
                preferred_element_type=jnp.float32,
            )
            total = term if total is None else total + term
    return total.astype(jnp.bfloat16)


def solution(mesh):
    fine = Mesh(np.asarray(mesh.devices).reshape(NZ, NY, NX, NC), ("z", "y", "x", "core"))
    store, head = ("z", "y"), ("x", "core")
    in_specs = (
        P(store, head),
        P(store, None),
        P(store, None, None, head),
        P(head, None),
    )
    return jax.shard_map(
        body, mesh=fine, in_specs=in_specs, out_specs=P(store, head), check_vma=False
    )
```

time: 645 us -> 470 us (0.73)
  waiting for transfers between devices: 487 us -> 225 us
  Pallas kernels: 0 us -> 58.5 us
  starting transfers between devices: 5.52 us -> 62 us
  local copies, waits for them, and re-layouts: 94.8 us -> 59.1 us
  matrix products: 18.6 us -> 32.9 us
    all_to_all x1 -> x11, waiting for transfers between devices: 380 us -> 224 us  [the longest x2 77.3 us: body(): kv_all.append(lax.all_to_all(both(own), 'y', 0, 0, tiled=True))]
    reduce_scatter x1 -> x0, waiting for transfers between devices: 107 us -> none  [body(): lax.psum_scatter(partial_value.astype(jnp.bfloat16), 'head', scatter_dime...]
    gather x4 -> x0, local copies, waits for them, and re-layouts: 73.5 us -> none  [the longest x2 50.7 us: body(): neighbour_kv[jnp.maximum(lax.all_to_all(requests, 'store', split_axis=0,...]
    pallas_call x0 -> x8, Pallas kernels: none -> 58.5 us  [the longest x4 50.9 us: attend(): pl.pallas_call(attn_kernel, grid_spec=pltpu.PrefetchScalarGridSpec(num_sc...]
    all_to_all x1 -> x11, starting transfers between devices: 5.3 us -> 53.3 us  [the longest x4 18.8 us: body(): back = lax.all_to_all(parts, 'z', 0, 0, tiled=True)]
    all_to_all x1 -> x0, blocking collectives: 20.4 us -> none  [body(): lax.all_to_all(requests, 'store', split_axis=0, concat_axis=0, tiled=True)]
    dynamic_slice x0 -> x3, local copies, waits for them, and re-layouts: none -> 20 us  [the longest x2 13.6 us: body(): w_send = lax.dynamic_index_in_dim(plane, 1 - cme, 2, keepdims=False)]
    unnamed x0 -> x1, blocking collectives: none -> 15.7 us
  transfers between devices with their start and end apart: 2 -> 18, of which waited for: 2 -> 10; matrix products, arithmetic and copies ran while one was open for 0% -> 13% of each run, Pallas kernels for 0% -> 12%
where the time goes in v1:
time: 470 us; the launch traced here: 468 us
  waiting for transfers between devices  225 us (48%)
  starting transfers between devices  62 us (13%)
  local copies, waits for them, and re-layouts  59.1 us (13%)
  Pallas kernels  58.5 us (12%)
  matrix products  32.9 us (7%)
  blocking collectives  15.7 us (3%)
  between operations  14.4 us (3%)
    all_to_all x2, waiting for transfers between devices, body(): kv_all.append(lax.all_to_all(both(own), 'y', 0, 0, tiled=True))  77.3 us
    all_to_all x1, waiting for transfers between devices, body(): plane = lax.all_to_all(shares, 'x', 0, 0, tiled=True)  59.8 us
    all_to_all x4, waiting for transfers between devices, body(): back = lax.all_to_all(parts, 'z', 0, 0, tiled=True)  58.9 us
    pallas_call x4, Pallas kernels, attend(): pl.pallas_call(attn_kernel, grid_spec=pltpu.PrefetchScalarGridSpec(num_sc...  50.9 us
    dot_general x8, matrix products, body(): lax.dot_general(ctx.reshape(NX * DH, -1), weight[:, rows].reshape(NX * DH...  32.9 us
    all_to_all x4, waiting for transfers between devices, body(): gathered = lax.all_to_all(context, 'x', 0, 0, tiled=True)  28.5 us
    unnamed x33, local copies, waits for them, and re-layouts  26.2 us
    all_to_all x4, starting transfers between devices, body(): back = lax.all_to_all(parts, 'z', 0, 0, tiled=True)  18.8 us
  transfers between devices with their start and end apart: 18, of which 10 were waited for; matrix products, arithmetic and copies ran while one was open for 13% of the time, Pallas kernels for 12%

profile of v1, /device:TPU:1, one launch (start us, length us, event | category | flops | bytes accessed | tf_op | source)
XLA Modules:
  0.0 468.0 jit_solution(10757316115557292786)
XLA Ops:
  14.6 5.1 %all-to-all-start.6 = ((bf16[4,2,2,8,128,128]{5,4,3,2,1,0:T(8,128)(2,1)}), bf16[4,2,2,8,128,128]{5,4,3,2,1,0:T(8,128)(2,1)}, u32[]{:S(2)}, u32[]{:S(2)}) async-start(bf16[4,2,2,8,128,128]{5,4,3,2,1,0:T(8,128)(2,1)} %broadcast_in_dim.5), calls=%async_computation.6 | async-start | bytes 8388608 | tf_op jit(solution)/shard_map/all_to_all | solution.py:173
  22.9 43.8 %all-to-all-done.6.kv_ref = bf16[4,2,2,8,128,128]{5,4,3,2,1,0:T(8,128)(2,1)} async-done(((bf16[4,2,2,8,128,128]{5,4,3,2,1,0:T(8,128)(2,1)}), bf16[4,2,2,8,128,128]{5,4,3,2,1,0:T(8,128)(2,1)}, u32[]{:S(2)}, u32[]{:S(2)}) %all-to-all-start.6) | async-done | bytes 4194336 | tf_op jit(solution)/shard_map/all_to_all | solution.py:173
  69.8 4.9 %all-to-all-start = ((bf16[4,2,2,8,128,128]{5,4,3,2,1,0:T(8,128)(2,1)}), bf16[4,2,2,8,128,128]{5,4,3,2,1,0:T(8,128)(2,1)}, u32[]{:S(2)}, u32[]{:S(2)}) async-start(bf16[4,2,2,8,128,128]{5,4,3,2,1,0:T(8,128)(2,1)} %broadcast_in_dim.4), calls=%async_computation | async-start | bytes 8388608 | tf_op jit(solution)/shard_map/all_to_all | solution.py:173
  74.6 11.9 %copy.21 = bf16[512,8192]{0,1:T(8,128)(2,1)} copy(bf16[512,8192]{1,0:T(8,128)(2,1)} %param.7) | data formatting | bytes 16777216 | tf_op args[3]
  86.6 33.5 %all-to-all-done.kv_ref = bf16[4,2,2,8,128,128]{5,4,3,2,1,0:T(8,128)(2,1)} async-done(((bf16[4,2,2,8,128,128]{5,4,3,2,1,0:T(8,128)(2,1)}), bf16[4,2,2,8,128,128]{5,4,3,2,1,0:T(8,128)(2,1)}, u32[]{:S(2)}, u32[]{:S(2)}) %all-to-all-start) | async-done | bytes 4194336 | tf_op jit(solution)/shard_map/all_to_all | solution.py:173
  120.1 7.9 %all-to-all-start.3 = ((bf16[4,512,2048]{1,2,0:T(8,128)(2,1)}), bf16[4,512,2048]{1,2,0:T(8,128)(2,1)}, u32[]{:S(2)}, u32[]{:S(2)}) async-start(bf16[4,512,2048]{1,2,0:T(8,128)(2,1)} %bitcast.70), calls=%async_computation.3 | async-start | bytes 16777216 | tf_op jit(solution)/shard_map/all_to_all | solution.py:175
  130.6 15.7 %all-reduce.ids_ref = s32[256]{0:T(256)S(1)} all-reduce(s32[256]{0:T(256)S(1)} %dynamic-update-slice), channel_id=1, replica_groups=mesh['z'=8,'y'=4,'x'=4,'core'=2] {'z'}, use_global_device_ids=true, to_apply=%add | all-reduce | flops 256 | bytes 2048
  148.6 12.7 %attend.6 = bf16[8,528,128]{2,1,0:T(8,128)(2,1)} custom-call(s32[256]{0:T(256)S(1)} %all-reduce.ids_ref, s32[1]{0:T(128)} %bitcast.1.me_ref, bf16[8192,256]{1,0:T(8,128)(2,1)S(1)} %copy-done, bf16[4,2,2,8,128,128]{5,4,3,2,1,0:T(8,128)(2,1)} %all-to-all-done.6.kv_ref), custom_call_target="tpu_custom_call" | custom-call | flops 2147483648 | bytes 8388608 | tf_op jit(solution)/shard_map/attend/pallas_call | solution.py:71
  161.4 59.8 %all-to-all-done.3 = bf16[4,512,2048]{1,2,0:T(8,128)(2,1)} async-done(((bf16[4,512,2048]{1,2,0:T(8,128)(2,1)}), bf16[4,512,2048]{1,2,0:T(8,128)(2,1)}, u32[]{:S(2)}, u32[]{:S(2)}) %all-to-all-start.3) | async-done | bytes 8388640 | tf_op jit(solution)/shard_map/all_to_all | solution.py:175
  221.1 8.1 %all-to-all-start.7 = ((bf16[8,528,128]{2,1,0:T(8,128)(2,1)}), bf16[8,528,128]{2,1,0:T(8,128)(2,1)S(1)}, u32[]{:S(2)}, u32[]{:S(2)}) async-start(bf16[8,528,128]{2,1,0:T(8,128)(2,1)} %attend.6), calls=%async_computation.7 | async-start | bytes 2162688 | tf_op jit(solution)/shard_map/all_to_all | solution.py:186
  231.5 12.7 %attend.7 = bf16[8,528,128]{2,1,0:T(8,128)(2,1)} custom-call(s32[256]{0:T(256)S(1)} %all-reduce.ids_ref, s32[1]{0:T(128)} %bitcast.1.me_ref, bf16[8192,256]{1,0:T(8,128)(2,1)S(1)} %copy-done.1, bf16[4,2,2,8,128,128]{5,4,3,2,1,0:T(8,128)(2,1)} %all-to-all-done.6.kv_ref), custom_call_target="tpu_custom_call" | custom-call | flops 2147483648 | bytes 8388608 | tf_op jit(solution)/shard_map/attend/pallas_call | solution.py:71
  244.2 11.9 %all-to-all-done.7.part_ref = bf16[8,528,128]{2,1,0:T(8,128)(2,1)S(1)} async-done(((bf16[8,528,128]{2,1,0:T(8,128)(2,1)}), bf16[8,528,128]{2,1,0:T(8,128)(2,1)S(1)}, u32[]{:S(2)}, u32[]{:S(2)}) %all-to-all-start.7) | async-done | bytes 1081376 | tf_op jit(solution)/shard_map/all_to_all | solution.py:186
  256.0 3.6 all-to-all-start.9
  261.8 12.7 %attend.4 = bf16[8,528,128]{2,1,0:T(8,128)(2,1)} custom-call(s32[256]{0:T(256)S(1)} %all-reduce.ids_ref, s32[1]{0:T(128)} %bitcast.1.me_ref, bf16[8192,256]{1,0:T(8,128)(2,1)S(1)} %copy-done.2, bf16[4,2,2,8,128,128]{5,4,3,2,1,0:T(8,128)(2,1)} %all-to-all-done.kv_ref), custom_call_target="tpu_custom_call" | custom-call | flops 2147483648 | bytes 8388608 | tf_op jit(solution)/shard_map/attend/pallas_call | solution.py:71
  274.5 11.8 %all-to-all-done.9.part_ref = bf16[8,528,128]{2,1,0:T(8,128)(2,1)S(1)} async-done(((bf16[8,528,128]{2,1,0:T(8,128)(2,1)}), bf16[8,528,128]{2,1,0:T(8,128)(2,1)S(1)}, u32[]{:S(2)}, u32[]{:S(2)}) %all-to-all-start.9) | async-done | bytes 1081376 | tf_op jit(solution)/shard_map/all_to_all | solution.py:186
  292.1 12.7 %attend.5 = bf16[8,528,128]{2,1,0:T(8,128)(2,1)} custom-call(s32[256]{0:T(256)S(1)} %all-reduce.ids_ref, s32[1]{0:T(128)} %bitcast.1.me_ref, bf16[8192,256]{1,0:T(8,128)(2,1)S(1)} %copy-done.3, bf16[4,2,2,8,128,128]{5,4,3,2,1,0:T(8,128)(2,1)} %all-to-all-done.kv_ref), custom_call_target="tpu_custom_call" | custom-call | flops 2147483648 | bytes 8388608 | tf_op jit(solution)/shard_map/attend/pallas_call | solution.py:71
  304.8 11.8 %all-to-all-done.1.part_ref = bf16[8,528,128]{2,1,0:T(8,128)(2,1)S(1)} async-done(((bf16[8,528,128]{2,1,0:T(8,128)(2,1)}), bf16[8,528,128]{2,1,0:T(8,128)(2,1)S(1)}, u32[]{:S(2)}, u32[]{:S(2)}) %all-to-all-start.1) | async-done | bytes 1081376 | tf_op jit(solution)/shard_map/all_to_all | solution.py:186
  316.6 3.6 all-to-all-start.4
  323.9 23.4 %all-to-all-done.4.part_ref = bf16[8,528,128]{2,1,0:T(8,128)(2,1)S(1)} async-done(((bf16[8,528,128]{2,1,0:T(8,128)(2,1)}), bf16[8,528,128]{2,1,0:T(8,128)(2,1)S(1)}, u32[]{:S(2)}, u32[]{:S(2)}) %all-to-all-start.4) | async-done | bytes 1081376 | tf_op jit(solution)/shard_map/all_to_all | solution.py:186
  347.3 4.4 all-to-all-start.8
  351.7 7.3 %constant_dynamic-slice_fusion = (bf16[4,512,1,1024]{1,3,2,0:T(8,128)(2,1)}, bf16[4,512,1,1024]{1,3,2,0:T(8,128)(2,1)}) fusion(bf16[4,512,2,1024]{1,3,2,0:T(8,128)(2,1)} %bitcast.10, s32[]{:T(128)S(6)} %select_n.8, s32[]{:T(128)S(6)} %select_n.7), kind=kLoop, calls=%fused_computation.27 | loop fusion | bytes 16777224 | tf_op jit(solution)/shard_map/jit(dynamic_index_in_dim)/dynamic_slice | solution.py:178
  359.1 6.3 %copy.24 = bf16[4,512,1,1024]{3,1,0,2:T(8,128)(2,1)} copy(bf16[4,512,1,1024]{1,3,2,0:T(8,128)(2,1)} %get-tuple-element.5) | data formatting | bytes 8388608 | tf_op jit(solution)/shard_map/jit(dynamic_index_in_dim)/dynamic_slice | solution.py:178
  371.0 4.3 all-to-all-start.10
  377.7 12.7 %all-to-all-done.10 = bf16[4,128,1024]{2,1,0:T(8,128)(2,1)} async-done(((bf16[4,128,1024]{2,1,0:T(8,128)(2,1)}), bf16[4,128,1024]{2,1,0:T(8,128)(2,1)}, u32[]{:S(2)}, u32[]{:S(2)}) %all-to-all-start.10) | async-done | bytes 1048608 | tf_op jit(solution)/shard_map/all_to_all | solution.py:188
  396.3 11.6 %all-to-all-done.5 = bf16[4,128,1024]{2,1,0:T(8,128)(2,1)S(1)} async-done(((bf16[4,128,1024]{2,1,0:T(8,128)(2,1)}), bf16[4,128,1024]{2,1,0:T(8,128)(2,1)S(1)}, u32[]{:S(2)}, u32[]{:S(2)}) %all-to-all-start.5) | async-done | bytes 1048608 | tf_op jit(solution)/shard_map/all_to_all | solution.py:188
  407.9 4.3 all-to-all-start.2
  412.1 6.4 %copy.22 = bf16[4,512,1,1024]{3,1,0,2:T(8,128)(2,1)} copy(bf16[4,512,1,1024]{1,3,2,0:T(8,128)(2,1)} %get-tuple-element.6) | data formatting | bytes 8388608 | tf_op jit(solution)/shard_map/jit(dynamic_index_in_dim)/dynamic_slice | solution.py:177
  421.1 4.2 all-to-all-done.2
  437.5 4.9 %fusion.4 = f32[1024,1024,1]{1,0,2:T(8,128)} fusion(bf16[4,128,1024]{2,1,0:T(8,128)(2,1)} %collective-permute-done.3, bf16[4,512,1024]{2,1,0:T(8,128)(2,1)} %collective-permute-done.1), kind=kOutput, calls=%fused_computation.11 | convolution fusion | flops 1073741824 | bytes 6291456 | tf_op jit(solution)/shard_map/dot_general | solution.py:192
  442.4 4.9 %fusion.8 = f32[1024,1024,1]{1,0,2:T(8,128)} fusion(bf16[4,128,1024]{2,1,0:T(8,128)(2,1)} %collective-permute-done.2, bf16[4,512,1024]{2,1,0:T(8,128)(2,1)} %collective-permute-done.1), kind=kOutput, calls=%fused_computation.15 | convolution fusion | flops 1073741824 | bytes 6291456 | tf_op jit(solution)/shard_map/dot_general | solution.py:192
  447.2 4.5 fusion.12
  451.7 9.5 %fusion = bf16[1024,1024]{1,0:T(8,128)(2,1)} fusion(f32[1024,1024,1]{1,0,2:T(8,128)S(1)} %fusion.2, f32[1024,1024,1]{1,0,2:T(8,128)} %fusion.4, f32[1024,1024,1]{1,0,2:T(8,128)S(1)} %fusion.6, f32[1024,1024,1]{1,0,2:T(8,128)} %fusion.8, f32[1024,1024,1]{1,0,2:T(8,128)S(1)} %fusion.10, f32[1024,1024,1]{1,0,2:T(8,128)} %fusion.12, ...), kind=kOutput, calls=%fused_computation.1 | convolution fusion | flops 1082130432 | bytes 33554432 | tf_op jit(solution)/shard_map/dot_general | solution.py:192
  (70 shorter events, 60.7 us)
Async XLA Ops:
  14.6 5.2 %copy-start.9 = (bf16[1024,512]{1,0:T(8,128)(2,1)S(1)}, bf16[1024,512]{1,0:T(8,128)(2,1)}, u32[]{:S(2)}) copy-start(bf16[1024,512]{1,0:T(8,128)(2,1)} %param.4) | copy-start | bytes 3145732
  14.6 52.1 %all-to-all-start.6 = ((bf16[4,2,2,8,128,128]{5,4,3,2,1,0:T(8,128)(2,1)}), bf16[4,2,2,8,128,128]{5,4,3,2,1,0:T(8,128)(2,1)}, u32[]{:S(2)}, u32[]{:S(2)}) async-start(bf16[4,2,2,8,128,128]{5,4,3,2,1,0:T(8,128)(2,1)} %broadcast_in_dim.5), calls=%async_computation.6 | async-start | bytes 8388608 | tf_op jit(solution)/shard_map/all_to_all | solution.py:173
  19.7 126.6 %all-gather.5.cloned.1.call-start = ((), (), s32[]{:S(2)}) async-start(), calls=%async_computation.12 | async-start | bytes 4718592 | tf_op jit(solution)/shard_map/all_gather | solution.py:166
  69.8 50.4 %all-to-all-start = ((bf16[4,2,2,8,128,128]{5,4,3,2,1,0:T(8,128)(2,1)}), bf16[4,2,2,8,128,128]{5,4,3,2,1,0:T(8,128)(2,1)}, u32[]{:S(2)}, u32[]{:S(2)}) async-start(bf16[4,2,2,8,128,128]{5,4,3,2,1,0:T(8,128)(2,1)} %broadcast_in_dim.4), calls=%async_computation | async-start | bytes 8388608 | tf_op jit(solution)/shard_map/all_to_all | solution.py:173
  120.1 8.7 %copy-start.10 = (s32[16,2]{0,1:T(2,128)S(1)}, s32[16,2]{0,1:T(2,128)}, u32[]{:S(2)}) copy-start(s32[16,2]{0,1:T(2,128)} %param.5) | copy-start | bytes 388
  120.1 8.9 %copy-start.11 = (u32[256]{0:T(256)S(1)}, u32[256]{0:T(256)}, u32[]{:S(2)}) copy-start(u32[256]{0:T(256)} %constant.26) | copy-start | bytes 3076
  120.1 101.0 %all-to-all-start.3 = ((bf16[4,512,2048]{1,2,0:T(8,128)(2,1)}), bf16[4,512,2048]{1,2,0:T(8,128)(2,1)}, u32[]{:S(2)}, u32[]{:S(2)}) async-start(bf16[4,512,2048]{1,2,0:T(8,128)(2,1)} %bitcast.70), calls=%async_computation.3 | async-start | bytes 16777216 | tf_op jit(solution)/shard_map/all_to_all | solution.py:175
  128.1 131.6 %all-gather.3.cloned.1.call-start = ((), (), s32[]{:S(2)}) async-start(), calls=%async_computation.11 | async-start | bytes 4718592 | tf_op jit(solution)/shard_map/all_gather | solution.py:166
  146.3 2.3 copy-start
  221.1 34.9 %all-to-all-start.7 = ((bf16[8,528,128]{2,1,0:T(8,128)(2,1)}), bf16[8,528,128]{2,1,0:T(8,128)(2,1)S(1)}, u32[]{:S(2)}, u32[]{:S(2)}) async-start(bf16[8,528,128]{2,1,0:T(8,128)(2,1)} %attend.6), calls=%async_computation.7 | async-start | bytes 2162688 | tf_op jit(solution)/shard_map/all_to_all | solution.py:186
  229.3 2.2 copy-start.1
  256.0 18.5 %copy-start.4 = (bf16[8,528,128]{2,1,0:T(8,128)(2,1)}, bf16[8,528,128]{2,1,0:T(8,128)(2,1)S(1)}, u32[]{:S(2)}) copy-start(bf16[8,528,128]{2,1,0:T(8,128)(2,1)S(1)} %all-to-all-done.7.part_ref) | copy-start | bytes 3244036
  256.0 30.3 %all-to-all-start.9 = ((bf16[8,528,128]{2,1,0:T(8,128)(2,1)}), bf16[8,528,128]{2,1,0:T(8,128)(2,1)S(1)}, u32[]{:S(2)}, u32[]{:S(2)}) async-start(bf16[8,528,128]{2,1,0:T(8,128)(2,1)} %attend.7), calls=%async_computation.9 | async-start | bytes 2162688 | tf_op jit(solution)/shard_map/all_to_all | solution.py:186
  259.6 2.2 copy-start.2
  286.3 30.3 %all-to-all-start.1 = ((bf16[8,528,128]{2,1,0:T(8,128)(2,1)}), bf16[8,528,128]{2,1,0:T(8,128)(2,1)S(1)}, u32[]{:S(2)}, u32[]{:S(2)}) async-start(bf16[8,528,128]{2,1,0:T(8,128)(2,1)} %attend.4), calls=%async_computation.1 | async-start | bytes 2162688 | tf_op jit(solution)/shard_map/all_to_all | solution.py:186
  289.9 2.2 copy-start.3
  316.6 30.7 %all-to-all-start.4 = ((bf16[8,528,128]{2,1,0:T(8,128)(2,1)}), bf16[8,528,128]{2,1,0:T(8,128)(2,1)S(1)}, u32[]{:S(2)}, u32[]{:S(2)}) async-start(bf16[8,528,128]{2,1,0:T(8,128)(2,1)} %attend.5), calls=%async_computation.4 | async-start | bytes 2162688 | tf_op jit(solution)/shard_map/all_to_all | solution.py:186
  320.2 1.2 copy-start.5
  322.9 1.0 copy-start.6
  347.3 23.7 %all-to-all-start.8 = ((bf16[4,128,1024]{2,1,0:T(8,128)(2,1)}), bf16[4,128,1024]{2,1,0:T(8,128)(2,1)}, u32[]{:S(2)}, u32[]{:S(2)}) async-start(bf16[4,128,1024]{2,1,0:T(8,128)(2,1)} %copy-done.6), calls=%async_computation.8 | async-start | bytes 2097152 | tf_op jit(solution)/shard_map/all_to_all | solution.py:188
  365.4 72.1 %collective-permute-start.1 = (bf16[4,512,1024]{2,1,0:T(8,128)(2,1)}, bf16[4,512,1024]{2,1,0:T(8,128)(2,1)}, u32[]{:S(2)}, u32[]{:S(2)}) collective-permute-start(bf16[4,512,1024]{2,1,0:T(8,128)(2,1)} %bitcast.75), channel_id=1, source_target_pairs={{0,1},{1,0},{2,3},{3,2},{4,5},{5,4},{6,7},{7,6},{8,9},{9,8},{10,11... | collective-permute-start | bytes 12582920 | tf_op jit(solution)/shard_map/ppermute | solution.py:180
  370.0 1.0 copy-start.7
  371.0 19.3 %all-to-all-start.10 = ((bf16[4,128,1024]{2,1,0:T(8,128)(2,1)}), bf16[4,128,1024]{2,1,0:T(8,128)(2,1)}, u32[]{:S(2)}, u32[]{:S(2)}) async-start(bf16[4,128,1024]{2,1,0:T(8,128)(2,1)} %copy-done.7), calls=%async_computation.10 | async-start | bytes 2097152 | tf_op jit(solution)/shard_map/all_to_all | solution.py:188
  390.4 17.5 %all-to-all-start.5 = ((bf16[4,128,1024]{2,1,0:T(8,128)(2,1)}), bf16[4,128,1024]{2,1,0:T(8,128)(2,1)S(1)}, u32[]{:S(2)}, u32[]{:S(2)}) async-start(bf16[4,128,1024]{2,1,0:T(8,128)(2,1)} %merge.5), calls=%async_computation.5 | async-start | bytes 2097152 | tf_op jit(solution)/shard_map/all_to_all | solution.py:188
  407.9 17.4 %all-to-all-start.2 = ((bf16[4,128,1024]{2,1,0:T(8,128)(2,1)}), bf16[4,128,1024]{2,1,0:T(8,128)(2,1)}, u32[]{:S(2)}, u32[]{:S(2)}) async-start(bf16[4,128,1024]{2,1,0:T(8,128)(2,1)} %merge.4), calls=%async_computation.2 | async-start | bytes 2097152 | tf_op jit(solution)/shard_map/all_to_all | solution.py:188
  418.5 33.2 %collective-permute-start.4 = (bf16[4,128,1024]{2,1,0:T(8,128)(2,1)}, bf16[4,128,1024]{2,1,0:T(8,128)(2,1)}, u32[]{:S(2)}, u32[]{:S(2)}) collective-permute-start(bf16[4,128,1024]{2,1,0:T(8,128)(2,1)} %all-to-all-done.10), channel_id=1, source_target_pairs={{0,1},{1,0},{2,3},{3,2},{4,5},{5,4},{6,7},{7,6},{8,9},{9,8},{10,11... | collective-permute-start | bytes 3145736 | tf_op jit(solution)/shard_map/ppermute | solution.py:189
  420.5 17.0 %collective-permute-start.3 = (bf16[4,128,1024]{2,1,0:T(8,128)(2,1)}, bf16[4,128,1024]{2,1,0:T(8,128)(2,1)}, u32[]{:S(2)}, u32[]{:S(2)}) collective-permute-start(bf16[4,128,1024]{2,1,0:T(8,128)(2,1)} %all-to-all-done.8), channel_id=1, source_target_pairs={{0,1},{1,0},{2,3},{3,2},{4,5},{5,4},{6,7},{7,6},{8,9},{9,8},{10,11... | collective-permute-start | bytes 3145736 | tf_op jit(solution)/shard_map/ppermute | solution.py:189
  420.6 21.8 %collective-permute-start.2 = (bf16[4,128,1024]{2,1,0:T(8,128)(2,1)S(1)}, bf16[4,128,1024]{2,1,0:T(8,128)(2,1)}, u32[]{:S(2)}, u32[]{:S(2)}) collective-permute-start(bf16[4,128,1024]{2,1,0:T(8,128)(2,1)S(1)} %all-to-all-done.5), channel_id=1, source_target_pairs={{0,1},{1,0},{2,3},{3,2},{4,5},{5,4},{6,7},{7,6},{8,9},{9,8},{10,11... | collective-permute-start | bytes 3145736 | tf_op jit(solution)/shard_map/ppermute | solution.py:189
  425.3 5.8 %copy-start.8 = (bf16[4,512,1,1024]{3,1,0,2:T(8,128)(2,1)S(1)}, bf16[4,512,1,1024]{3,1,0,2:T(8,128)(2,1)}, u32[]{:S(2)}) copy-start(bf16[4,512,1,1024]{3,1,0,2:T(8,128)(2,1)} %copy.22) | copy-start | bytes 12582916
  425.3 22.0 %collective-permute-start = (bf16[4,128,1024]{2,1,0:T(8,128)(2,1)}, bf16[4,128,1024]{2,1,0:T(8,128)(2,1)S(1)}, u32[]{:S(2)}, u32[]{:S(2)}) collective-permute-start(bf16[4,128,1024]{2,1,0:T(8,128)(2,1)} %all-to-all-done.2), channel_id=1, source_target_pairs={{0,1},{1,0},{2,3},{3,2},{4,5},{5,4},{6,7},{7,6},{8,9},{9,8},{10,11... | collective-permute-start | bytes 3145736 | tf_op jit(solution)/shard_map/ppermute | solution.py:189
Sparse Core Ops, SparseCore 0:
  22.3 58.7 all-gather.4
  130.7 59.6 all-gather.2

commit v2 on v0

v2 whole, which is shorter than its diff:
```python
import jax
import jax.numpy as jnp
import numpy as np
from jax import lax
from jax.experimental import pallas as pl
from jax.experimental.pallas import tpu as pltpu
from jax.sharding import Mesh, PartitionSpec as P

NZ, NY, NX, NC = 8, 4, 4, 2
DH = 128
SEG = 64
SEGS = 16
ROWS = SEG * SEGS
REFS = 2 * SEGS
NB_DEV = 8
NB_LEN = 128
NB_BITS = 3
CAP = 2
PAIR = CAP * SEG
TAIL = 32
PART = NZ * DH + TAIL
MB = 1 << 20


def attn_kernel(plan_ref, *refs):
    q_refs, (kv_ref, out_ref, lse_ref) = refs[:NY], refs[NY:]
    zi = pl.program_id(0)
    yme = plan_ref[NZ * NY * CAP]
    low = lax.broadcasted_iota(jnp.int32, (1, PAIR), 1) < SEG
    nt = (((1,), (1,)), ((), ()))
    scores, values = [], []
    for a in range(NY):
        queries, keys = [], []
        for r in range(CAP):
            code = plan_ref[(zi * NY + a) * CAP + r]
            at = code & (NB_DEV - 1)
            start = pl.multiple_of((code >> NB_BITS) * SEG, SEG)
            queries.append(q_refs[a][pl.ds(start, SEG), :])
            keys.append(kv_ref[0, at])
            values.append(kv_ref[1, at])
        values[-2:] = [jnp.concatenate(values[-2:], axis=0)]
        pair = jnp.concatenate(queries, axis=0)
        keys = jnp.concatenate(keys, axis=0)
        both = lax.dot_general(keys, pair, nt, preferred_element_type=jnp.float32)
        scores.append(jnp.where(low, both[:NB_LEN], both[NB_LEN:]))
    scores = jnp.concatenate(scores, axis=1) * (DH**-0.5)
    top = jnp.max(scores, axis=0, keepdims=True)
    weights = jnp.exp(scores - top)
    total = jnp.sum(weights, axis=0, keepdims=True)
    rounded = weights.astype(jnp.bfloat16)
    inverse = 1.0 / total
    lse = top + jnp.log(total)
    hi = lse.astype(jnp.bfloat16).astype(jnp.float32)
    mid = (lse - hi).astype(jnp.bfloat16).astype(jnp.float32)
    lo = lse - hi - mid
    start = pl.multiple_of(zi * DH, DH)
    for a in range(NY):
        at = slice(a * PAIR, (a + 1) * PAIR)
        both = jnp.dot(values[a], rounded[:, at], preferred_element_type=jnp.float32)
        out = (jnp.where(low, both[:DH], both[DH:]) * inverse[:, at]).astype(jnp.bfloat16)
        out_ref[(yme + a) & (NY - 1), pl.ds(start, DH), :] = out
        for k, piece in enumerate((hi, mid, lo)):
            lse_ref[a, pl.ds(k * NZ + zi, 1), :] = piece[:, at]

    @pl.when(zi == NZ - 1)
    def _():
        for a in range(NY):
            lse_ref[a, 3 * NZ :, :] = jnp.zeros((TAIL - 3 * NZ, PAIR), jnp.float32)
            tail = lse_ref[a].astype(jnp.bfloat16)
            out_ref[(yme + a) & (NY - 1), NZ * DH :, :] = tail


def attend(plan, q_blocks, kv, head, at):
    sq = pl.Squeezed()
    return pl.pallas_call(
        attn_kernel,
        grid_spec=pltpu.PrefetchScalarGridSpec(
            num_scalar_prefetch=1,
            grid=(NZ,),
            in_specs=[pl.BlockSpec((ROWS, DH), lambda z, *_: (0, head))] * NY
            + [pl.BlockSpec((sq, sq, 2, NB_DEV, DH, DH), lambda z, *_: (z, at, 0, 0, 0, 0))],
            out_specs=pl.BlockSpec((NY, PART, PAIR), lambda z, *_: (0, 0, 0)),
            scratch_shapes=[pltpu.VMEM((NY, TAIL, PAIR), jnp.float32)],
        ),
        out_shape=jax.ShapeDtypeStruct((NY, PART, PAIR), jnp.bfloat16),
        compiler_params=pltpu.CompilerParams(vmem_limit_bytes=48 * MB),
        cost_estimate=pl.CostEstimate(
            flops=32 * 4 * 2 * DH**3 * 4, bytes_accessed=20 * MB, transcendentals=32 * DH * DH
        ),
        name="attend",
    )(plan, *q_blocks, kv)


def merge_kernel(place_ref, part_ref, out_ref, lse_ref):
    for y in range(NY):
        tail = part_ref[y, NZ * DH :, :].astype(jnp.float32)
        lse_ref[y] = tail[0:NZ] + tail[NZ : 2 * NZ] + tail[2 * NZ : 3 * NZ]
    low = lax.broadcasted_iota(jnp.int32, (1, PAIR), 1) < SEG
    for p in range(SEGS // 2):
        sums, lses = [], []
        for j in range(2):
            halves_o, halves_l = [], []
            for side in range(2):
                code = place_ref[2 * (2 * p + side) + j]
                half, y, z = code & 1, (code >> 1) & (NY - 1), code >> 3
                start = pl.multiple_of(z * DH, DH)
                part = part_ref[y, pl.ds(start, DH), :].astype(jnp.float32)
                lse = lse_ref[y, pl.ds(z, 1), :]
                shift = jnp.where(half == side, 0, SEG)
                halves_o.append(pltpu.roll(part, shift, 1))
                halves_l.append(pltpu.roll(lse, shift, 1))
            sums.append(jnp.where(low, halves_o[0], halves_o[1]))
            lses.append(jnp.where(low, halves_l[0], halves_l[1]))
        top = jnp.maximum(lses[0], lses[1])
        f0, f1 = jnp.exp(lses[0] - top), jnp.exp(lses[1] - top)
        scale = 1.0 / (f0 + f1)
        context = (f0 * scale) * sums[0] + (f1 * scale) * sums[1]
        out_ref[p * PAIR : (p + 1) * PAIR, :] = jnp.transpose(context).astype(jnp.bfloat16)


def merge(place, parts):
    return pl.pallas_call(
        merge_kernel,
        grid_spec=pltpu.PrefetchScalarGridSpec(
            num_scalar_prefetch=1,
            grid=(),
            in_specs=[pl.BlockSpec(memory_space=pltpu.VMEM)],
            out_specs=pl.BlockSpec(memory_space=pltpu.VMEM),
            scratch_shapes=[pltpu.VMEM((NY, NZ, PAIR), jnp.float32)],
        ),
        out_shape=jax.ShapeDtypeStruct((ROWS, DH), jnp.bfloat16),
        compiler_params=pltpu.CompilerParams(vmem_limit_bytes=16 * MB),
        cost_estimate=pl.CostEstimate(
            flops=8 * DH * ROWS, bytes_accessed=8 * MB, transcendentals=2 * ROWS
        ),
        name="merge",
    )(place, parts)


def project(contexts, weights, head, total, last):
    groups = len(contexts)
    cols = weights[0].shape[1]
    width = 256
    first = total is None

    def kernel(*refs):
        ctx, wgt = refs[:groups], refs[groups : 2 * groups]
        out_ref = refs[-1]
        left = jnp.concatenate([ref[...] for ref in ctx], axis=1)
        right = jnp.concatenate([ref[...] for ref in wgt], axis=0)
        term = jnp.dot(left, right, preferred_element_type=jnp.float32)
        if not first:
            term = term + refs[2 * groups][...]
        out_ref[...] = term.astype(out_ref.dtype)

    block = pl.BlockSpec((ROWS, width), lambda n: (0, n))
    in_specs = [pl.BlockSpec((ROWS, DH), lambda n: (0, 0))] * groups
    in_specs += [pl.BlockSpec((DH, width), lambda n: (head, n))] * groups
    operands = [*contexts, *weights]
    if not first:
        in_specs.append(block)
        operands.append(total)
    return pl.pallas_call(
        kernel,
        grid=(cols // width,),
        in_specs=in_specs,
        out_specs=block,
        out_shape=jax.ShapeDtypeStruct((ROWS, cols), jnp.bfloat16 if last else jnp.float32),
        input_output_aliases={} if first or last else {2 * groups: 0},
        compiler_params=pltpu.CompilerParams(vmem_limit_bytes=16 * MB),
        cost_estimate=pl.CostEstimate(
            flops=2 * ROWS * cols * groups * DH, bytes_accessed=12 * MB, transcendentals=0
        ),
        name="project",
    )(*operands)


def ring(axis, size, step):
    return [(i, (i + step) % size) for i in range(size)]


def earlier_equal(keys):
    order = jnp.arange(keys.shape[-1])
    same = keys[..., :, None] == keys[..., None, :]
    return jnp.sum((same & (order[None, :] < order[:, None])).astype(jnp.int32), axis=-1)


def body(queries, neighbour_ids, neighbour_kv, out_weight):
    heads = queries.shape[1] // DH
    yme, xme, cme = (lax.axis_index(a).astype(jnp.int32) for a in ("y", "x", "core"))
    cols = out_weight.shape[1] // (NX * NC)
    barrier = lax.optimization_barrier

    split = heads - 1
    block = neighbour_kv.reshape(NB_DEV, NB_LEN, 2, heads, DH)
    keys = jnp.transpose(block[:, :, 0], (2, 0, 1, 3))
    values = jnp.transpose(block[:, :, 1], (2, 0, 3, 1))
    own = jnp.stack([keys, values], axis=1)
    kv_first = lax.all_gather(own[:split], "z")
    kv_last = lax.all_gather(own[split:], "z")

    chip_cols = NC * cols
    shares = []
    for dx in range(NX):
        target = (xme + dx) % NX
        share = lax.dynamic_slice_in_dim(out_weight, target * chip_cols, chip_cols, 1)
        shares.append(lax.ppermute(share, "x", ring("x", NX, dx)) if dx else share)

    q_all = [queries] + [lax.ppermute(queries, "y", ring("y", NY, -d)) for d in range(1, NY)]

    ids = neighbour_ids.reshape(-1)
    ids_row = lax.all_gather(ids, "y")
    asked = jnp.roll(ids_row, -yme, axis=0)
    holder = asked >> NB_BITS
    rank = earlier_equal(holder)
    want = (jnp.arange(NZ) * NY + yme)[:, None, None, None]
    hit = (holder[None, :, None, :] == want) & (
        rank[None, :, None, :] == jnp.arange(CAP)[None, None, :, None]
    )
    code = (jnp.arange(REFS) // 2) * NB_DEV + (asked & (NB_DEV - 1))
    plan = jnp.sum(jnp.where(hit, code[None, :, None, :], 0), axis=-1).reshape(-1)
    plan = jnp.concatenate([plan, yme.reshape(1)])
    mine = ids >> NB_BITS
    place = mine * CAP + earlier_equal(mine)

    swap = [(0, 1), (1, 0)]
    weights = []
    for share in shares:
        keep = lax.dynamic_slice_in_dim(share, cme * cols, cols, 1)
        rest = lax.dynamic_slice_in_dim(share, (1 - cme) * cols, cols, 1)
        weights += [keep, lax.ppermute(rest, "core", swap)]

    kv_first, q_all, weights, plan, place = barrier((kv_first, q_all, weights, plan, place))

    def near(context):
        return [context] + [lax.ppermute(context, "x", ring("x", NX, d)) for d in range(1, NX)]

    def both_cores(came):
        return [c for own in came for c in (own, lax.ppermute(own, "core", swap))]

    def after(value, *others):
        return barrier((value, others))[0]

    def send(parts):
        return lax.all_to_all(parts, "y", 0, 0, tiled=True)

    parts0 = attend(plan, q_all, kv_first, 0, 0)
    back0 = send(parts0)
    parts1 = attend(plan, q_all, kv_first, 1, 1)
    back1 = send(parts1)
    parts2 = attend(after(plan, parts1), q_all, kv_first, 2, 2)
    context0 = merge(place, after(back0, parts2))
    came0 = near(context0)
    back2 = send(after(parts2, came0))
    context1 = merge(place, after(back1, came0))
    came1 = near(context1)
    parts3 = attend(plan, q_all, after(kv_last, context1), 3, 0)
    back3 = send(after(parts3, came1))
    full0 = both_cores(came0)
    context2 = merge(place, after(back2, parts3))
    came2 = near(context2)
    total = project(after(full0, context2), weights, 0, None, False)
    total = project(both_cores(came1), weights, 1, total, False)
    context3 = merge(place, after(back3, came2, total))
    came3 = near(context3)
    total = project(both_cores(after(came2, context3)), weights, 2, total, False)
    came3[1:] = after(came3[1:], total)
    return project(both_cores(came3), weights, 3, total, True)


def solution(mesh):
    fine = Mesh(np.asarray(mesh.devices).reshape(NZ, NY, NX, NC), ("z", "y", "x", "core"))
    store, head = ("z", "y"), ("x", "core")
    in_specs = (
        P(store, head),
        P(store, None),
        P(store, None, None, head),
        P(head, None),
    )
    return jax.shard_map(
        body, mesh=fine, in_specs=in_specs, out_specs=P(store, head), check_vma=False
    )
```

time: 645 us -> 302 us (0.47)
  waiting for transfers between devices: 487 us -> 87.9 us
  Pallas kernels: 0 us -> 60.3 us
  starting transfers between devices: 5.52 us -> 63.4 us
  local copies, waits for them, and re-layouts: 94.8 us -> 44.9 us
  matrix products: 18.6 us -> 0 us
  blocking collectives: 20.4 us -> 27.5 us
    all_to_all x1 -> x4, waiting for transfers between devices: 380 us -> 6.2 us  [send(): return lax.all_to_all(parts, 'y', 0, 0, tiled=True)]
    reduce_scatter x1 -> x0, waiting for transfers between devices: 107 us -> none  [body(): lax.psum_scatter(partial_value.astype(jnp.bfloat16), 'head', scatter_dime...]
    gather x4 -> x0, local copies, waits for them, and re-layouts: 73.5 us -> none  [the longest x2 50.7 us: body(): neighbour_kv[jnp.maximum(lax.all_to_all(requests, 'store', split_axis=0,...]
    ppermute x0 -> x38, waiting for transfers between devices: none -> 70.5 us  [the longest x3 45.3 us: body(): shares.append(lax.ppermute(share, 'x', ring('x', NX, dx)) if dx else share)]
    pallas_call x0 -> x12, Pallas kernels: none -> 60.3 us  [the longest x4 30.3 us: attend(): pl.pallas_call(attn_kernel, grid_spec=pltpu.PrefetchScalarGridSpec(num_sc...]
    ppermute x0 -> x38, starting transfers between devices: none -> 45.9 us  [the longest x12 16.6 us: near(): lax.ppermute(context, 'x', ring('x', NX, d))]
    all_gather x0 -> x1, blocking collectives: none -> 27.5 us  [body(): ids_row = lax.all_gather(ids, 'y')]
    all_to_all x1 -> x0, blocking collectives: 20.4 us -> none  [body(): lax.all_to_all(requests, 'store', split_axis=0, concat_axis=0, tiled=True)]
  transfers between devices with their start and end apart: 2 -> 44, of which waited for: 2 -> 11; matrix products, arithmetic and copies ran while one was open for 0% -> 7% of each run, Pallas kernels for 0% -> 18%
where the time goes in v2:
time: 302 us; the launch traced here: 300 us
  waiting for transfers between devices  87.9 us (29%)
  starting transfers between devices  63.4 us (21%)
  Pallas kernels  60.3 us (20%)
  local copies, waits for them, and re-layouts  44.9 us (15%)
  blocking collectives  27.5 us (9%)
  between operations  13.8 us (5%)
    ppermute x3, waiting for transfers between devices, body(): shares.append(lax.ppermute(share, 'x', ring('x', NX, dx)) if dx else share)  45.3 us
    pallas_call x4, Pallas kernels, attend(): pl.pallas_call(attn_kernel, grid_spec=pltpu.PrefetchScalarGridSpec(num_sc...  30.3 us
    all_gather x1, blocking collectives, body(): ids_row = lax.all_gather(ids, 'y')  27.5 us
    unnamed x44, local copies, waits for them, and re-layouts  23.5 us
    pallas_call x4, Pallas kernels, project(): pl.pallas_call(kernel, grid=(cols // width,), in_specs=in_specs, out_spec...  19.4 us
    all_to_all x4, starting transfers between devices, send(): return lax.all_to_all(parts, 'y', 0, 0, tiled=True)  17.5 us
    ppermute x12, starting transfers between devices, near(): lax.ppermute(context, 'x', ring('x', NX, d))  16.6 us
    ppermute x3, waiting for transfers between devices, body(): lax.ppermute(queries, 'y', ring('y', NY, -d))  14.3 us
  transfers between devices with their start and end apart: 44, of which 11 were waited for; matrix products, arithmetic and copies ran while one was open for 7% of the time, Pallas kernels for 18%

profile of v2, /device:TPU:1, one launch (start us, length us, event | category | flops | bytes accessed | tf_op | source)
XLA Modules:
  0.0 299.7 jit_solution(9893102138523124693)
XLA Ops:
  6.5 6.2 %copy.21 = bf16[8,128,2,512]{1,3,2,0:T(8,128)(2,1)} copy(bf16[8,128,2,512]{3,2,1,0:T(2,128)(2,1)} %param.6) | data formatting | bytes 4194304 | tf_op args[2]
  17.5 5.9 %constant_dynamic-slice_fusion.3 = (bf16[512,2048]{1,0:T(8,128)(2,1)}, bf16[512,2048]{1,0:T(8,128)(2,1)S(1)}, bf16[512,2048]{1,0:T(8,128)(2,1)}) fusion(bf16[512,8192]{1,0:T(8,128)(2,1)} %param.7, s32[]{:T(128)S(6)} %select_n.86, s32[]{:T(128)S(6)} %select_n.82, s32[]{:T(128)S(6)} %select_n.84), kind=kLoop, calls=%fused_computation.16 | loop fusion | bytes 12582924 | tf_op jit(solution)/shard_map/dynamic_slice | solution.py:206
  29.0 3.6 %constant_dynamic-slice_fusion.10 = (bf16[512,1024]{1,0:T(8,128)(2,1)}, bf16[512,1024]{1,0:T(8,128)(2,1)S(1)}) fusion(bf16[512,8192]{1,0:T(8,128)(2,1)} %param.7, s32[]{:T(128)S(6)} %dynamic_slice.46, s32[]{:T(128)S(6)} %dynamic_slice.44), kind=kLoop, calls=%fused_computation.23 | loop fusion | bytes 4194312 | tf_op jit(solution)/shard_map/dynamic_slice | solution.py:230
  34.2 2.7 collective-permute-start
  37.1 27.5 %all-gather.2 = s32[4,1,32]{2,1,0:T(1,128)S(1)} all-gather(s32[1,1,32]{2,1,0:T(1,128)S(1)} %reshape.76), channel_id=1, replica_groups=mesh['z'=8,'y'=4,'x'=4,'core'=2] {'y'}, dimensions={0}, use_global_device_ids=true | all-gather | bytes 640 | tf_op jit(solution)/shard_map/all_gather | solution.py:212
  64.8 5.0 %collective-permute-done.4 = bf16[512,2048]{1,0:T(8,128)(2,1)} collective-permute-done((bf16[512,2048]{1,0:T(8,128)(2,1)S(1)}, bf16[512,2048]{1,0:T(8,128)(2,1)}, u32[]{:S(2)}, u32[]{:S(2)}) %collective-permute-start.4) | collective-permute-done | bytes 2097184 | tf_op jit(solution)/shard_map/ppermute | solution.py:207
  69.8 5.1 %collective-permute-start.1 = (bf16[1024,512]{1,0:T(8,128)(2,1)}, bf16[1024,512]{1,0:T(8,128)(2,1)}, u32[]{:S(2)}, u32[]{:S(2)}) collective-permute-start(bf16[1024,512]{1,0:T(8,128)(2,1)} %refs_0_.3), channel_id=1, source_target_pairs={{0,16},{8,24},{16,0},{24,8},{1,17},{9,25},{17,1},{25,9},{2,18},{10... | collective-permute-start | bytes 3145736 | tf_op jit(solution)/shard_map/ppermute | solution.py:209
  74.9 2.7 constant_dynamic-slice_fusion.7
  77.7 40.3 %collective-permute-done.6 = bf16[512,2048]{1,0:T(8,128)(2,1)} collective-permute-done((bf16[512,2048]{1,0:T(8,128)(2,1)}, bf16[512,2048]{1,0:T(8,128)(2,1)}, u32[]{:S(2)}, u32[]{:S(2)}) %collective-permute-start.6) | collective-permute-done | bytes 2097184 | tf_op jit(solution)/shard_map/ppermute | solution.py:207
  119.2 2.7 constant_dynamic-slice_fusion.4
  123.8 3.1 %constant_dynamic-slice_fusion.1 = (bf16[512,1024]{1,0:T(8,128)(2,1)}, bf16[512,1024]{1,0:T(8,128)(2,1)}) fusion(bf16[512,2048]{1,0:T(8,128)(2,1)} %collective-permute-done.8, s32[]{:T(128)S(6)} %select_n.79, s32[]{:T(128)S(6)} %select_n.74), kind=kLoop, calls=%fused_computation.14 | loop fusion | bytes 4194312 | tf_op jit(solution)/shard_map/dynamic_slice | solution.py:230
  128.4 14.3 %collective-permute-done.2.refs_3_ = bf16[1024,512]{1,0:T(8,128)(2,1)} collective-permute-done((bf16[1024,512]{1,0:T(8,128)(2,1)}, bf16[1024,512]{1,0:T(8,128)(2,1)}, u32[]{:S(2)}, u32[]{:S(2)}) %collective-permute-start.2) | collective-permute-done | bytes 1048608 | tf_op jit(solution)/shard_map/ppermute | solution.py:209
  142.7 11.2 %all-gather.6.cloned.1.call-done = bf16[24,2,8,128,128]{4,3,2,1,0:T(8,128)(2,1)} async-done(((bf16[3,2,8,128,128]{4,3,2,1,0:T(8,128)(2,1)}), bf16[24,2,8,128,128]{4,3,2,1,0:T(8,128)(2,1)}) %all-gather.6.cloned.1.call-update) | async-done | bytes 12582928 | tf_op jit(solution)/shard_map/all_gather | solution.py:199
  153.9 7.6 %attend.5 = bf16[4,1056,128]{2,1,0:T(8,128)(2,1)S(1)} custom-call(s32[65]{0:T(128)S(1)} %pad_add_fusion.1.plan_ref, bf16[1024,512]{1,0:T(8,128)(2,1)} %refs_0_.3, bf16[1024,512]{1,0:T(8,128)(2,1)} %collective-permute-done.refs_1_, bf16[1024,512]{1,0:T(8,128)(2,1)} %collective-permute-done.1.refs_2_, bf16[1024,512]{1,0:T(8,128)(2,1)} %collective-permute-done.2.refs_3_, ...), custom_call_target="tpu_custom_call" | custom-call | flops 2147483648 | bytes 20971520 | tf_op jit(solution)/shard_map/attend/pallas_call | solution.py:75
  162.5 4.3 %all-to-all-start.1 = ((bf16[4,1056,128]{2,1,0:T(8,128)(2,1)}), bf16[4,1056,128]{2,1,0:T(8,128)(2,1)}, u32[]{:S(2)}, u32[]{:S(2)}) async-start(bf16[4,1056,128]{2,1,0:T(8,128)(2,1)} %copy-done.8), calls=%async_computation.1 | async-start | bytes 2162688 | tf_op jit(solution)/shard_map/all_to_all | solution.py:245
  166.8 7.6 %attend.4 = bf16[4,1056,128]{2,1,0:T(8,128)(2,1)S(1)} custom-call(s32[65]{0:T(128)S(1)} %pad_add_fusion.1.plan_ref, bf16[1024,512]{1,0:T(8,128)(2,1)} %refs_0_.3, bf16[1024,512]{1,0:T(8,128)(2,1)} %collective-permute-done.refs_1_, bf16[1024,512]{1,0:T(8,128)(2,1)} %collective-permute-done.1.refs_2_, bf16[1024,512]{1,0:T(8,128)(2,1)} %collective-permute-done.2.refs_3_, ...), custom_call_target="tpu_custom_call" | custom-call | flops 2147483648 | bytes 20971520 | tf_op jit(solution)/shard_map/attend/pallas_call | solution.py:75
  175.3 6.2 %all-to-all-done.1.part_ref = bf16[4,1056,128]{2,1,0:T(8,128)(2,1)} async-done(((bf16[4,1056,128]{2,1,0:T(8,128)(2,1)}), bf16[4,1056,128]{2,1,0:T(8,128)(2,1)}, u32[]{:S(2)}, u32[]{:S(2)}) %all-to-all-start.1) | async-done | bytes 1081376 | tf_op jit(solution)/shard_map/all_to_all | solution.py:245
  181.5 4.4 %all-to-all-start = ((bf16[4,1056,128]{2,1,0:T(8,128)(2,1)}), bf16[4,1056,128]{2,1,0:T(8,128)(2,1)}, u32[]{:S(2)}, u32[]{:S(2)}) async-start(bf16[4,1056,128]{2,1,0:T(8,128)(2,1)} %copy-done.7), calls=%async_computation | async-start | bytes 2162688 | tf_op jit(solution)/shard_map/all_to_all | solution.py:245
  186.0 7.6 %attend.6 = bf16[4,1056,128]{2,1,0:T(8,128)(2,1)S(1)} custom-call(s32[65]{0:T(128)S(1)} %pad_add_fusion.1.plan_ref, bf16[1024,512]{1,0:T(8,128)(2,1)} %refs_0_.3, bf16[1024,512]{1,0:T(8,128)(2,1)} %collective-permute-done.refs_1_, bf16[1024,512]{1,0:T(8,128)(2,1)} %collective-permute-done.1.refs_2_, bf16[1024,512]{1,0:T(8,128)(2,1)} %collective-permute-done.2.refs_3_, ...), custom_call_target="tpu_custom_call" | custom-call | flops 2147483648 | bytes 20971520 | tf_op jit(solution)/shard_map/attend/pallas_call | solution.py:75
  194.6 2.5 merge.4.refs_0_
  202.0 2.7 collective-permute-done.10.refs_2_
  204.7 6.4 %collective-permute-done.11.refs_4_ = bf16[1024,128]{1,0:T(8,128)(2,1)S(1)} collective-permute-done((bf16[1024,128]{1,0:T(8,128)(2,1)S(1)}, bf16[1024,128]{1,0:T(8,128)(2,1)S(1)}, u32[]{:S(2)}, u32[]{:S(2)}) %collective-permute-start.11) | collective-permute-done | bytes 262176 | tf_op jit(solution)/shard_map/ppermute | solution.py:236
  211.8 4.3 %all-to-all-start.3 = ((bf16[4,1056,128]{2,1,0:T(8,128)(2,1)}), bf16[4,1056,128]{2,1,0:T(8,128)(2,1)}, u32[]{:S(2)}, u32[]{:S(2)}) async-start(bf16[4,1056,128]{2,1,0:T(8,128)(2,1)} %copy-done.6), calls=%async_computation.3 | async-start | bytes 2162688 | tf_op jit(solution)/shard_map/all_to_all | solution.py:245
  216.1 3.2 %merge.5.refs_0_ = bf16[1024,128]{1,0:T(8,128)(2,1)} custom-call(s32[32]{0:T(128)S(1)} %multiply_add_fusion.place_ref, bf16[4,1056,128]{2,1,0:T(8,128)(2,1)} %all-to-all-done.part_ref), custom_call_target="tpu_custom_call" | custom-call | flops 1048576 | bytes 8388608 | tf_op jit(solution)/shard_map/merge/pallas_call | solution.py:122
  223.6 3.0 %collective-permute-start.23 = (bf16[1024,128]{1,0:T(8,128)(2,1)S(1)}, bf16[1024,128]{1,0:T(8,128)(2,1)}, u32[]{:S(2)}, u32[]{:S(2)}) collective-permute-start(bf16[1024,128]{1,0:T(8,128)(2,1)S(1)} %merge.4.refs_0_), channel_id=1, source_target_pairs={{0,1},{1,0},{2,3},{3,2},{4,5},{5,4},{6,7},{7,6},{8,9},{9,8},{10,11... | collective-permute-start | bytes 786440 | tf_op jit(solution)/shard_map/ppermute | solution.py:239
  226.6 7.6 %attend.7 = bf16[4,1056,128]{2,1,0:T(8,128)(2,1)S(1)} custom-call(s32[65]{0:T(128)S(1)} %pad_add_fusion.1.plan_ref, bf16[1024,512]{1,0:T(8,128)(2,1)} %refs_0_.3, bf16[1024,512]{1,0:T(8,128)(2,1)} %collective-permute-done.refs_1_, bf16[1024,512]{1,0:T(8,128)(2,1)} %collective-permute-done.1.refs_2_, bf16[1024,512]{1,0:T(8,128)(2,1)} %collective-permute-done.2.refs_3_, ...), custom_call_target="tpu_custom_call" | custom-call | flops 2147483648 | bytes 20971520 | tf_op jit(solution)/shard_map/attend/pallas_call | solution.py:75
  235.2 4.5 %all-to-all-start.2 = ((bf16[4,1056,128]{2,1,0:T(8,128)(2,1)}), bf16[4,1056,128]{2,1,0:T(8,128)(2,1)}, u32[]{:S(2)}, u32[]{:S(2)}) async-start(bf16[4,1056,128]{2,1,0:T(8,128)(2,1)} %copy-done.5), calls=%async_computation.2 | async-start | bytes 2162688 | tf_op jit(solution)/shard_map/all_to_all | solution.py:245
  252.4 4.6 %project.4.refs_16_ = f32[1024,1024]{1,0:T(8,128)S(1)} custom-call(bf16[1024,128]{1,0:T(8,128)(2,1)S(1)} %merge.4.refs_0_, bf16[1024,128]{1,0:T(8,128)(2,1)} %collective-permute-done.23.refs_1_, bf16[1024,128]{1,0:T(8,128)(2,1)S(1)} %copy-done.12, bf16[1024,128]{1,0:T(8,128)(2,1)S(1)} %collective-permute-done.24.refs_3_, bf16[1024,128]{1,0:T(8,128)(2,1)S(1)} %copy-done.14, ...), custom_call_target="tpu_custom_call" | custom-call | flops 2147483648 | bytes 12582912 | tf_op jit(solution)/shard_map/project/pallas_call | solution.py:163
  257.0 4.9 %project.5.refs_16_ = f32[1024,1024]{1,0:T(8,128)S(1)} custom-call(bf16[1024,128]{1,0:T(8,128)(2,1)} %merge.5.refs_0_, bf16[1024,128]{1,0:T(8,128)(2,1)S(1)} %collective-permute-done.19.refs_1_, bf16[1024,128]{1,0:T(8,128)(2,1)} %collective-permute-done.13.refs_2_, ...), custom_call_target="tpu_custom_call", output_to_operand_aliasing={{}: (16, {})} | custom-call | flops 2147483648 | bytes 12582912 | tf_op jit(solution)/shard_map/project/pallas_call | solution.py:163
  265.4 2.5 merge.7.refs_0_
  279.7 4.6 %project.6.refs_16_ = f32[1024,1024]{1,0:T(8,128)S(1)} custom-call(bf16[1024,128]{1,0:T(8,128)(2,1)S(1)} %copy-done.10, bf16[1024,128]{1,0:T(8,128)(2,1)S(1)} %collective-permute-done.31.refs_1_, bf16[1024,128]{1,0:T(8,128)(2,1)S(1)} %copy-done.16, bf16[1024,128]{1,0:T(8,128)(2,1)S(1)} %collective-permute-done.32.refs_3_, ...), custom_call_target="tpu_custom_call", output_to_operand_aliasing={{}: (16, {})} | custom-call | flops 2147483648 | bytes 12582912 | tf_op jit(solution)/shard_map/project/pallas_call | solution.py:163
  287.6 5.2 %project.7 = bf16[1024,1024]{1,0:T(8,128)(2,1)} custom-call(bf16[1024,128]{1,0:T(8,128)(2,1)S(1)} %merge.7.refs_0_, bf16[1024,128]{1,0:T(8,128)(2,1)S(1)} %collective-permute-done.27.refs_1_, bf16[1024,128]{1,0:T(8,128)(2,1)S(1)} %collective-permute-done.28.refs_2_, bf16[1024,128]{1,0:T(8,128)(2,1)S(1)} %collective-permute-done.35.refs_3_, ...), custom_call_target="tpu_custom_call" | custom-call | flops 2147483648 | bytes 12582912 | tf_op jit(solution)/shard_map/project/pallas_call | solution.py:163
  (141 shorter events, 62.0 us)
Async XLA Ops:
  6.5 147.4 %all-gather.6.cloned.1.call-start = ((), (), s32[]{:S(2)}) async-start(), calls=%async_computation.4 | async-start | bytes 14155776 | tf_op jit(solution)/shard_map/all_gather | solution.py:199
  16.5 210.1 %all-gather.8.cloned.1.call-start = ((), (), s32[]{:S(2)}) async-start(), calls=%async_computation.5 | async-start | bytes 4718592 | tf_op jit(solution)/shard_map/all_gather | solution.py:200
  23.4 46.5 %collective-permute-start.4 = (bf16[512,2048]{1,0:T(8,128)(2,1)S(1)}, bf16[512,2048]{1,0:T(8,128)(2,1)}, u32[]{:S(2)}, u32[]{:S(2)}) collective-permute-start(bf16[512,2048]{1,0:T(8,128)(2,1)S(1)} %get-tuple-element.82), channel_id=1, source_target_pairs={{0,2},{2,4},{4,6},{6,0},{1,3},{3,5},{5,7},{7,1},{8,10},{10,12},{12... | collective-permute-start | bytes 6291464 | tf_op jit(solution)/shard_map/ppermute | solution.py:207
  25.4 92.5 %collective-permute-start.6 = (bf16[512,2048]{1,0:T(8,128)(2,1)}, bf16[512,2048]{1,0:T(8,128)(2,1)}, u32[]{:S(2)}, u32[]{:S(2)}) collective-permute-start(bf16[512,2048]{1,0:T(8,128)(2,1)} %get-tuple-element.83), channel_id=1, source_target_pairs={{0,4},{2,6},{4,0},{6,2},{1,5},{3,7},{5,1},{7,3},{8,12},{10,14},{12... | collective-permute-start | bytes 6291464 | tf_op jit(solution)/shard_map/ppermute | solution.py:207
  27.9 94.1 %collective-permute-start.8 = (bf16[512,2048]{1,0:T(8,128)(2,1)}, bf16[512,2048]{1,0:T(8,128)(2,1)}, u32[]{:S(2)}, u32[]{:S(2)}) collective-permute-start(bf16[512,2048]{1,0:T(8,128)(2,1)} %get-tuple-element.81), channel_id=1, source_target_pairs={{0,6},{2,0},{4,2},{6,4},{1,7},{3,1},{5,3},{7,5},{8,14},{10,8},{12,... | collective-permute-start | bytes 6291464 | tf_op jit(solution)/shard_map/ppermute | solution.py:207
  32.7 94.2 %collective-permute-start.3 = (bf16[512,1024]{1,0:T(8,128)(2,1)}, bf16[512,1024]{1,0:T(8,128)(2,1)}, u32[]{:S(2)}, u32[]{:S(2)}) collective-permute-start(bf16[512,1024]{1,0:T(8,128)(2,1)} %get-tuple-element.84), channel_id=1, source_target_pairs={{0,1},{1,0},{2,3},{3,2},{4,5},{5,4},{6,7},{7,6},{8,9},{9,8},{10,11... | collective-permute-start | bytes 3145736 | tf_op jit(solution)/shard_map/ppermute | solution.py:231
  34.2 92.7 %collective-permute-start = (bf16[1024,512]{1,0:T(8,128)(2,1)}, bf16[1024,512]{1,0:T(8,128)(2,1)}, u32[]{:S(2)}, u32[]{:S(2)}) collective-permute-start(bf16[1024,512]{1,0:T(8,128)(2,1)} %refs_0_.3), channel_id=1, source_target_pairs={{0,24},{8,0},{16,8},{24,16},{1,25},{9,1},{17,9},{25,17},{2,26},{10... | collective-permute-start | bytes 3145736 | tf_op jit(solution)/shard_map/ppermute | solution.py:209
  69.8 58.6 %collective-permute-start.1 = (bf16[1024,512]{1,0:T(8,128)(2,1)}, bf16[1024,512]{1,0:T(8,128)(2,1)}, u32[]{:S(2)}, u32[]{:S(2)}) collective-permute-start(bf16[1024,512]{1,0:T(8,128)(2,1)} %refs_0_.3), channel_id=1, source_target_pairs={{0,16},{8,24},{16,0},{24,8},{1,17},{9,25},{17,1},{25,9},{2,18},{10... | collective-permute-start | bytes 3145736 | tf_op jit(solution)/shard_map/ppermute | solution.py:209
  117.9 24.8 %collective-permute-start.2 = (bf16[1024,512]{1,0:T(8,128)(2,1)}, bf16[1024,512]{1,0:T(8,128)(2,1)}, u32[]{:S(2)}, u32[]{:S(2)}) collective-permute-start(bf16[1024,512]{1,0:T(8,128)(2,1)} %refs_0_.3), channel_id=1, source_target_pairs={{0,8},{8,16},{16,24},{24,0},{1,9},{9,17},{17,25},{25,1},{2,10},{10... | collective-permute-start | bytes 3145736 | tf_op jit(solution)/shard_map/ppermute | solution.py:209
  121.9 20.7 %collective-permute-start.5 = (bf16[512,1024]{1,0:T(8,128)(2,1)}, bf16[512,1024]{1,0:T(8,128)(2,1)}, u32[]{:S(2)}, u32[]{:S(2)}) collective-permute-start(bf16[512,1024]{1,0:T(8,128)(2,1)} %get-tuple-element.90), channel_id=1, source_target_pairs={{0,1},{1,0},{2,3},{3,2},{4,5},{5,4},{6,7},{7,6},{8,9},{9,8},{10,11... | collective-permute-start | bytes 3145736 | tf_op jit(solution)/shard_map/ppermute | solution.py:231
  126.9 15.8 %collective-permute-start.7 = (bf16[512,1024]{1,0:T(8,128)(2,1)}, bf16[512,1024]{1,0:T(8,128)(2,1)}, u32[]{:S(2)}, u32[]{:S(2)}) collective-permute-start(bf16[512,1024]{1,0:T(8,128)(2,1)} %get-tuple-element.88), channel_id=1, source_target_pairs={{0,1},{1,0},{2,3},{3,2},{4,5},{5,4},{6,7},{7,6},{8,9},{9,8},{10,11... | collective-permute-start | bytes 3145736 | tf_op jit(solution)/shard_map/ppermute | solution.py:231
  126.9 15.8 %collective-permute-start.9 = (bf16[512,1024]{1,0:T(8,128)(2,1)}, bf16[512,1024]{1,0:T(8,128)(2,1)}, u32[]{:S(2)}, u32[]{:S(2)}) collective-permute-start(bf16[512,1024]{1,0:T(8,128)(2,1)} %get-tuple-element.86), channel_id=1, source_target_pairs={{0,1},{1,0},{2,3},{3,2},{4,5},{5,4},{6,7},{7,6},{8,9},{9,8},{10,11... | collective-permute-start | bytes 3145736 | tf_op jit(solution)/shard_map/ppermute | solution.py:231
  162.5 19.0 %all-to-all-start.1 = ((bf16[4,1056,128]{2,1,0:T(8,128)(2,1)}), bf16[4,1056,128]{2,1,0:T(8,128)(2,1)}, u32[]{:S(2)}, u32[]{:S(2)}) async-start(bf16[4,1056,128]{2,1,0:T(8,128)(2,1)} %copy-done.8), calls=%async_computation.1 | async-start | bytes 2162688 | tf_op jit(solution)/shard_map/all_to_all | solution.py:245
  181.5 30.3 %all-to-all-start = ((bf16[4,1056,128]{2,1,0:T(8,128)(2,1)}), bf16[4,1056,128]{2,1,0:T(8,128)(2,1)}, u32[]{:S(2)}, u32[]{:S(2)}) async-start(bf16[4,1056,128]{2,1,0:T(8,128)(2,1)} %copy-done.7), calls=%async_computation | async-start | bytes 2162688 | tf_op jit(solution)/shard_map/all_to_all | solution.py:245
  197.1 7.5 %collective-permute-start.10 = (bf16[1024,128]{1,0:T(8,128)(2,1)S(1)}, bf16[1024,128]{1,0:T(8,128)(2,1)S(1)}, u32[]{:S(2)}, u32[]{:S(2)}) collective-permute-start(bf16[1024,128]{1,0:T(8,128)(2,1)S(1)} %merge.4.refs_0_), channel_id=1, source_target_pairs={{0,2},{2,4},{4,6},{6,0},{1,3},{3,5},{5,7},{7,1},{8,10},{10,12},{12... | collective-permute-start | bytes 786440 | tf_op jit(solution)/shard_map/ppermute | solution.py:236
  198.4 12.7 %collective-permute-start.11 = (bf16[1024,128]{1,0:T(8,128)(2,1)S(1)}, bf16[1024,128]{1,0:T(8,128)(2,1)S(1)}, u32[]{:S(2)}, u32[]{:S(2)}) collective-permute-start(bf16[1024,128]{1,0:T(8,128)(2,1)S(1)} %merge.4.refs_0_), channel_id=1, source_target_pairs={{0,4},{2,6},{4,0},{6,2},{1,5},{3,7},{5,1},{7,3},{8,12},{10,14},{12... | collective-permute-start | bytes 786440 | tf_op jit(solution)/shard_map/ppermute | solution.py:236
  200.8 11.0 %collective-permute-start.12 = (bf16[1024,128]{1,0:T(8,128)(2,1)S(1)}, bf16[1024,128]{1,0:T(8,128)(2,1)}, u32[]{:S(2)}, u32[]{:S(2)}) collective-permute-start(bf16[1024,128]{1,0:T(8,128)(2,1)S(1)} %merge.4.refs_0_), channel_id=1, source_target_pairs={{0,6},{2,0},{4,2},{6,4},{1,7},{3,1},{5,3},{7,5},{8,14},{10,8},{12,... | collective-permute-start | bytes 786440 | tf_op jit(solution)/shard_map/ppermute | solution.py:236
  211.8 23.4 %all-to-all-start.3 = ((bf16[4,1056,128]{2,1,0:T(8,128)(2,1)}), bf16[4,1056,128]{2,1,0:T(8,128)(2,1)}, u32[]{:S(2)}, u32[]{:S(2)}) async-start(bf16[4,1056,128]{2,1,0:T(8,128)(2,1)} %copy-done.6), calls=%async_computation.3 | async-start | bytes 2162688 | tf_op jit(solution)/shard_map/all_to_all | solution.py:245
  219.3 15.9 %collective-permute-start.13 = (bf16[1024,128]{1,0:T(8,128)(2,1)}, bf16[1024,128]{1,0:T(8,128)(2,1)}, u32[]{:S(2)}, u32[]{:S(2)}) collective-permute-start(bf16[1024,128]{1,0:T(8,128)(2,1)} %merge.5.refs_0_), channel_id=1, source_target_pairs={{0,2},{2,4},{4,6},{6,0},{1,3},{3,5},{5,7},{7,1},{8,10},{10,12},{12... | collective-permute-start | bytes 786440 | tf_op jit(solution)/shard_map/ppermute | solution.py:236
  221.2 14.0 %collective-permute-start.14 = (bf16[1024,128]{1,0:T(8,128)(2,1)}, bf16[1024,128]{1,0:T(8,128)(2,1)}, u32[]{:S(2)}, u32[]{:S(2)}) collective-permute-start(bf16[1024,128]{1,0:T(8,128)(2,1)} %merge.5.refs_0_), channel_id=1, source_target_pairs={{0,4},{2,6},{4,0},{6,2},{1,5},{3,7},{5,1},{7,3},{8,12},{10,14},{12... | collective-permute-start | bytes 786440 | tf_op jit(solution)/shard_map/ppermute | solution.py:236
  223.4 11.8 %collective-permute-start.15 = (bf16[1024,128]{1,0:T(8,128)(2,1)}, bf16[1024,128]{1,0:T(8,128)(2,1)}, u32[]{:S(2)}, u32[]{:S(2)}) collective-permute-start(bf16[1024,128]{1,0:T(8,128)(2,1)} %merge.5.refs_0_), channel_id=1, source_target_pairs={{0,6},{2,0},{4,2},{6,4},{1,7},{3,1},{5,3},{7,5},{8,14},{10,8},{12,... | collective-permute-start | bytes 786440 | tf_op jit(solution)/shard_map/ppermute | solution.py:236
  223.6 18.0 %collective-permute-start.23 = (bf16[1024,128]{1,0:T(8,128)(2,1)S(1)}, bf16[1024,128]{1,0:T(8,128)(2,1)}, u32[]{:S(2)}, u32[]{:S(2)}) collective-permute-start(bf16[1024,128]{1,0:T(8,128)(2,1)S(1)} %merge.4.refs_0_), channel_id=1, source_target_pairs={{0,1},{1,0},{2,3},{3,2},{4,5},{5,4},{6,7},{7,6},{8,9},{9,8},{10,11... | collective-permute-start | bytes 786440 | tf_op jit(solution)/shard_map/ppermute | solution.py:239
  235.2 30.2 %all-to-all-start.2 = ((bf16[4,1056,128]{2,1,0:T(8,128)(2,1)}), bf16[4,1056,128]{2,1,0:T(8,128)(2,1)}, u32[]{:S(2)}, u32[]{:S(2)}) async-start(bf16[4,1056,128]{2,1,0:T(8,128)(2,1)} %copy-done.5), calls=%async_computation.2 | async-start | bytes 2162688 | tf_op jit(solution)/shard_map/all_to_all | solution.py:245
  242.4 14.6 %collective-permute-start.21 = (bf16[1024,128]{1,0:T(8,128)(2,1)}, bf16[1024,128]{1,0:T(8,128)(2,1)S(1)}, u32[]{:S(2)}, u32[]{:S(2)}) collective-permute-start(bf16[1024,128]{1,0:T(8,128)(2,1)} %collective-permute-done.14.refs_4_), channel_id=1, source_target_pairs={{0,1},{1,0},{2,3},{3,2},{4,5},{5,4},{6,7},{7,6},{8,9},{9,8},{10,11... | collective-permute-start | bytes 786440 | tf_op jit(solution)/shard_map/ppermute | solution.py:239
  242.8 14.2 %collective-permute-start.22 = (bf16[1024,128]{1,0:T(8,128)(2,1)}, bf16[1024,128]{1,0:T(8,128)(2,1)S(1)}, u32[]{:S(2)}, u32[]{:S(2)}) collective-permute-start(bf16[1024,128]{1,0:T(8,128)(2,1)} %collective-permute-done.15.refs_6_), channel_id=1, source_target_pairs={{0,1},{1,0},{2,3},{3,2},{4,5},{5,4},{6,7},{7,6},{8,9},{9,8},{10,11... | collective-permute-start | bytes 786440 | tf_op jit(solution)/shard_map/ppermute | solution.py:239
  245.7 18.3 %collective-permute-start.16 = (bf16[1024,128]{1,0:T(8,128)(2,1)S(1)}, bf16[1024,128]{1,0:T(8,128)(2,1)S(1)}, u32[]{:S(2)}, u32[]{:S(2)}) collective-permute-start(bf16[1024,128]{1,0:T(8,128)(2,1)S(1)} %merge.6.refs_0_), channel_id=1, source_target_pairs={{0,2},{2,4},{4,6},{6,0},{1,3},{3,5},{5,7},{7,1},{8,10},{10,12},{12... | collective-permute-start | bytes 786440 | tf_op jit(solution)/shard_map/ppermute | solution.py:236
  246.5 17.4 %collective-permute-start.17 = (bf16[1024,128]{1,0:T(8,128)(2,1)S(1)}, bf16[1024,128]{1,0:T(8,128)(2,1)S(1)}, u32[]{:S(2)}, u32[]{:S(2)}) collective-permute-start(bf16[1024,128]{1,0:T(8,128)(2,1)S(1)} %merge.6.refs_0_), channel_id=1, source_target_pairs={{0,4},{2,6},{4,0},{6,2},{1,5},{3,7},{5,1},{7,3},{8,12},{10,14},{12... | collective-permute-start | bytes 786440 | tf_op jit(solution)/shard_map/ppermute | solution.py:236
  248.7 16.7 %collective-permute-start.18 = (bf16[1024,128]{1,0:T(8,128)(2,1)S(1)}, bf16[1024,128]{1,0:T(8,128)(2,1)}, u32[]{:S(2)}, u32[]{:S(2)}) collective-permute-start(bf16[1024,128]{1,0:T(8,128)(2,1)S(1)} %merge.6.refs_0_), channel_id=1, source_target_pairs={{0,6},{2,0},{4,2},{6,4},{1,7},{3,1},{5,3},{7,5},{8,14},{10,8},{12,... | collective-permute-start | bytes 786440 | tf_op jit(solution)/shard_map/ppermute | solution.py:236
  269.6 14.8 %collective-permute-start.28 = (bf16[1024,128]{1,0:T(8,128)(2,1)S(1)}, bf16[1024,128]{1,0:T(8,128)(2,1)S(1)}, u32[]{:S(2)}, u32[]{:S(2)}) collective-permute-start(bf16[1024,128]{1,0:T(8,128)(2,1)S(1)} %merge.7.refs_0_), channel_id=1, source_target_pairs={{0,2},{2,4},{4,6},{6,0},{1,3},{3,5},{5,7},{7,1},{8,10},{10,12},{12... | collective-permute-start | bytes 786440 | tf_op jit(solution)/shard_map/ppermute | solution.py:236
  270.5 13.9 %collective-permute-start.29 = (bf16[1024,128]{1,0:T(8,128)(2,1)S(1)}, bf16[1024,128]{1,0:T(8,128)(2,1)S(1)}, u32[]{:S(2)}, u32[]{:S(2)}) collective-permute-start(bf16[1024,128]{1,0:T(8,128)(2,1)S(1)} %merge.7.refs_0_), channel_id=1, source_target_pairs={{0,4},{2,6},{4,0},{6,2},{1,5},{3,7},{5,1},{7,3},{8,12},{10,14},{12... | collective-permute-start | bytes 786440 | tf_op jit(solution)/shard_map/ppermute | solution.py:236
  271.6 12.8 %collective-permute-start.30 = (bf16[1024,128]{1,0:T(8,128)(2,1)S(1)}, bf16[1024,128]{1,0:T(8,128)(2,1)S(1)}, u32[]{:S(2)}, u32[]{:S(2)}) collective-permute-start(bf16[1024,128]{1,0:T(8,128)(2,1)S(1)} %merge.7.refs_0_), channel_id=1, source_target_pairs={{0,6},{2,0},{4,2},{6,4},{1,7},{3,1},{5,3},{7,5},{8,14},{10,8},{12,... | collective-permute-start | bytes 786440 | tf_op jit(solution)/shard_map/ppermute | solution.py:236
  273.4 12.8 %collective-permute-start.27 = (bf16[1024,128]{1,0:T(8,128)(2,1)S(1)}, bf16[1024,128]{1,0:T(8,128)(2,1)S(1)}, u32[]{:S(2)}, u32[]{:S(2)}) collective-permute-start(bf16[1024,128]{1,0:T(8,128)(2,1)S(1)} %merge.7.refs_0_), channel_id=1, source_target_pairs={{0,1},{1,0},{2,3},{3,2},{4,5},{5,4},{6,7},{7,6},{8,9},{9,8},{10,11... | collective-permute-start | bytes 786440 | tf_op jit(solution)/shard_map/ppermute | solution.py:239
  (32 other events, 108.8 us)
Sparse Core Ops, SparseCore 0:
  16.6 137.2 all-gather.5
  155.7 53.4 all-gather.7
